TPU v7x, 32 devices: a whole 2x2x4 slice. The times are simulated.
32 devices in a mesh: rays: 8 (over y, x, core), planes: 4 (over z).
Axes of the slice: x: 2, y: 2, z: 4, core: 2. Of those that a mesh axis runs over, the one named last changes fastest.
Arguments:
- tile_density: bfloat16 [4, 256, 128, 128], P(None, 'rays', 'planes'), may hold values from -6 to 6
- long_maps: bfloat16 [8, 4, 512, 2, 512], P('rays'), may hold values from -1.796875 to 1.796875
- map_owner: int32 [4], replicated, may hold values from 0 to 7
- tile_lists: int32 [8, 4, 64], replicated, may hold values from 0 to 255, as said below
- block_slots: int32 [4, 512], P(None, ('rays', 'planes')), may hold values from 0 to 63
- block_windows: int32 [4, 2, 512], P(None, None, ('rays', 'planes')), may hold values from 0 to 384
- fine_cells: int32 [4, 2, 262144], P(None, None, ('rays', 'planes')), may hold values from 0 to 126
- long_cells: int32 [4, 2, 262144], P(None, None, ('rays', 'planes')), may hold values from 0 to 126
- fractions: float32 [4, 4, 262144], P(None, None, ('rays', 'planes')), may hold values from 0 to 1
Outputs:
- deflection: float32 [4, 2, 262144], P(None, None, ('rays', 'planes'))
- source_shift: float32 [2, 262144], P(None, ('rays', 'planes'))
Inputs may be any that keep to these rules, and one draw needn't show every extreme that they name: `tile_lists`: tile t belongs to owner t // 32. In each list of one bundle and plane at most 16 entries name tiles of one owner, and some owner has exactly 16 entries in every such list; entries may repeat.
All inputs are finite; a program needn't handle non-finite values.
Results may differ from a plain program's by a relative error of at most 0.0064.
Values may be sent and summed in bfloat16 or wider, within the bound.
A program may use at most 128 MiB of HBM per device.

v0:
```python
import jax
import jax.numpy as jnp
from jax import lax
from jax.sharding import PartitionSpec as P

RATIO = 16


def spread(x, axis, root):
    mine = lax.axis_index(axis) == root
    return lax.psum(jnp.where(mine, x, jnp.zeros_like(x)), axis)


def kernel_tables(side):
    indices = jnp.arange(side, dtype=jnp.int32)
    offset = (indices[:, None] - indices[None, :]).astype(jnp.float32)
    tap_offsets = jnp.arange(-6, 7, dtype=jnp.int32).astype(jnp.float32)
    tap_total = jnp.sum(jnp.exp(-tap_offsets * tap_offsets / 8.0))
    inside = jnp.abs(offset) <= 6.0
    weight = jnp.where(inside, jnp.exp(-offset * offset / 8.0), 0.0) / tap_total
    smooth_table = weight.astype(jnp.bfloat16)
    slope_table = (6.0 * offset * weight / 4.0).astype(jnp.bfloat16)
    return (smooth_table, slope_table)


def convolve(density, smooth_table, slope_table):
    side = density.shape[1]
    right_table = jnp.concatenate([smooth_table.T, slope_table.T], axis=1)
    partial_value = jnp.einsum(
        "lij,jk->lik", density, right_table, preferred_element_type=jnp.float32
    ).astype(jnp.bfloat16)
    along_rows = jnp.einsum(
        "ij,ljk->lik", slope_table, partial_value[:, :, :side], preferred_element_type=jnp.float32
    )
    along_cols = jnp.einsum(
        "ij,ljk->lik", smooth_table, partial_value[:, :, side:], preferred_element_type=jnp.float32
    )
    return jnp.concatenate([along_rows, along_cols], axis=2).astype(jnp.bfloat16)


def interpolate(lookup, cell_row, cell_col, frac_row, frac_col):
    side = lookup.shape[1]
    positions = jnp.arange(side, dtype=jnp.int32)
    row_weight = jnp.where(positions == cell_row[..., None], 1.0 - frac_row[..., None], 0.0)
    row_weight = row_weight + jnp.where(
        positions == cell_row[..., None] + 1, frac_row[..., None], 0.0
    )
    col_weight = jnp.where(positions == cell_col[..., None], 1.0 - frac_col[..., None], 0.0)
    col_weight = col_weight + jnp.where(
        positions == cell_col[..., None] + 1, frac_col[..., None], 0.0
    )
    row_values = jnp.einsum(
        "bns,bsk->bnk", row_weight.astype(jnp.bfloat16), lookup, preferred_element_type=jnp.float32
    )
    along_x = jnp.sum(row_values[..., :side] * col_weight, axis=-1)
    along_y = jnp.sum(row_values[..., side:] * col_weight, axis=-1)
    return (along_x, along_y)


def map_windows(map_full, starts, side):

    def one_window(row_start, col_start):
        window = lax.dynamic_slice(map_full, (row_start, jnp.int32(0), col_start), (side, 2, side))
        return window.reshape(side, 2 * side)

    return jax.vmap(one_window)(starts[0], starts[1])


def lens_shift(previous, target, template):
    shifts = jnp.zeros_like(template)
    for earlier_plane, deflect in enumerate(previous[:target]):
        shifts = shifts - (target - earlier_plane) / target * deflect
    return shifts


def plane_step(fine_lookup, long_lookup, fine_cell, long_cell, offsets, shifts):
    fine_x, fine_y = interpolate(
        fine_lookup, fine_cell[0], fine_cell[1], offsets[0] + shifts[0], offsets[1] + shifts[1]
    )
    long_x, long_y = interpolate(
        long_lookup,
        long_cell[0],
        long_cell[1],
        offsets[2] + shifts[0] / RATIO,
        offsets[3] + shifts[1] / RATIO,
    )
    return jnp.stack([fine_x + long_x, fine_y + long_y])


def fetch_strips(store_rows, plane_lists, my_row, ray_count, capacity):
    tile_dev = store_rows.shape[0]
    list_len = plane_lists.shape[1]
    owners = plane_lists // tile_dev
    local_index = plane_lists % tile_dev
    list_positions = jnp.arange(list_len, dtype=jnp.int32)
    earlier = list_positions[:, None] > list_positions[None, :]
    same_owner = owners[:, :, None] == owners[:, None, :]
    rank_in_owner = jnp.sum(jnp.logical_and(same_owner, earlier[None]), axis=2)
    slot_ids = jnp.arange(capacity, dtype=jnp.int32)
    chosen = jnp.logical_and(
        owners[:, :, None] == my_row, rank_in_owner[:, :, None] == slot_ids[None, None, :]
    )
    send_index = jnp.sum(jnp.where(chosen, local_index[:, :, None], 0), axis=1)
    outgoing = jnp.take(store_rows, send_index.reshape(-1), axis=0)
    outgoing = outgoing.reshape(ray_count, capacity, store_rows.shape[1], store_rows.shape[2])
    incoming = lax.all_to_all(outgoing, "rays", split_axis=0, concat_axis=0, tiled=True)
    mine_owner = lax.dynamic_index_in_dim(owners, my_row, 0, keepdims=False)
    mine_rank = lax.dynamic_index_in_dim(rank_in_owner, my_row, 0, keepdims=False)
    flat_incoming = incoming.reshape(ray_count * capacity, store_rows.shape[1], store_rows.shape[2])
    return jnp.take(flat_incoming, mine_owner * capacity + mine_rank, axis=0)


def per_device(
    tile_density,
    long_maps,
    map_owner,
    tile_lists,
    block_slots,
    block_windows,
    fine_cells,
    long_cells,
    fractions,
):
    ray_count = lax.axis_size("rays")
    my_row = lax.axis_index("rays")
    tile_side = tile_density.shape[3]
    list_len = tile_lists.shape[2]
    capacity = 2 * list_len // ray_count
    plane_count = tile_density.shape[0]
    rays_here = fine_cells.shape[2]
    blocks = block_slots.shape[1]
    block_width = rays_here // blocks
    smooth_table, slope_table = kernel_tables(tile_side)
    fine_blocks = fine_cells.reshape(plane_count, 2, blocks, block_width)
    long_blocks = long_cells.reshape(plane_count, 2, blocks, block_width)
    frac_blocks = fractions.reshape(plane_count, 4, blocks, block_width)
    deflection_list = []
    for plane_index in range(plane_count):
        strip_rows = fetch_strips(
            tile_density[plane_index], tile_lists[:, plane_index, :], my_row, ray_count, capacity
        )
        full_tiles = lax.all_gather(strip_rows, "planes", axis=1, tiled=True)
        fields = convolve(full_tiles, smooth_table, slope_table)
        map_full = spread(long_maps[0, plane_index], "rays", map_owner[plane_index])
        fine_lookup = jnp.take(fields, block_slots[plane_index], axis=0)
        long_lookup = map_windows(map_full, block_windows[plane_index], tile_side)
        shifts = lens_shift(deflection_list, plane_index, frac_blocks[plane_index][:2])
        deflection_list.append(
            plane_step(
                fine_lookup,
                long_lookup,
                fine_blocks[plane_index],
                long_blocks[plane_index],
                frac_blocks[plane_index],
                shifts,
            )
        )
    source = lens_shift(deflection_list, plane_count, frac_blocks[0][:2])
    deflection = jnp.stack(deflection_list).reshape(plane_count, 2, rays_here)
    return (deflection, source.reshape(2, rays_here))


def solution(mesh):
    return jax.shard_map(
        per_device,
        mesh=mesh,
        in_specs=(
            P(None, "rays", "planes", None),
            P("rays", None, None, None, None),
            P(),
            P(),
            P(None, ("rays", "planes")),
            P(None, None, ("rays", "planes")),
            P(None, None, ("rays", "planes")),
            P(None, None, ("rays", "planes")),
            P(None, None, ("rays", "planes")),
        ),
        out_specs=(P(None, None, ("rays", "planes")), P(None, ("rays", "planes"))),
        check_vma=False,
    )
```

profile of v0, /device:TPU:0, one launch (start us, length us, event | category | flops | bytes accessed | tf_op | source)
XLA Modules:
  0.0 465.2 jit_solution(8058626936329648664)
XLA Ops:
  12.1 6.2 %fusion.99 = (bf16[512,2,512]{2,1,0:T(2,128)(2,1)}, bf16[512,2,512]{2,1,0:T(2,128)(2,1)}, bf16[512,2,512]{2,1,0:T(2,128)(2,1)}, bf16[512,2,512]{2,1,0:T(2,128)(2,1)}) fusion(pred[]{:T(512)S(6)} %eq.756, bf16[1,4,512,2,512]{4,3,2,1,0:T(2,128)(2,1)} %param.16, pred[]{:T(512)S(6)} %eq.682, pred[]{:T(512)S(6)} %eq.645, pred[]{:T(512)S(6)} %eq.719), kind=kLoop, calls=%fused_computation.191 | loop fusion | flops 2097152 | bytes 8388612 | tf_op jit(solution)/shard_map/jit(_where)/select_n | solution.py:11
  22.8 5.2 %all-to-all-start = ((bf16[8,16,32,128]{3,2,1,0:T(8,128)(2,1)}), bf16[8,16,32,128]{3,2,1,0:T(8,128)(2,1)S(1)}, u32[]{:S(2)}, u32[]{:S(2)}) async-start(bf16[8,16,32,128]{3,2,1,0:T(8,128)(2,1)} %bitcast.5), calls=%async_computation | async-start | bytes 2097152 | tf_op jit(solution)/shard_map/all_to_all | solution.py:106
  28.0 26.8 %all-to-all-done = bf16[8,16,32,128]{3,2,1,0:T(8,128)(2,1)S(1)} async-done(((bf16[8,16,32,128]{3,2,1,0:T(8,128)(2,1)}), bf16[8,16,32,128]{3,2,1,0:T(8,128)(2,1)S(1)}, u32[]{:S(2)}, u32[]{:S(2)}) %all-to-all-start) | async-done | bytes 1048608 | tf_op jit(solution)/shard_map/all_to_all | solution.py:106
  58.5 3.7 all-to-all-start.1
  64.1 3.3 slice_reduce_fusion.1
  71.8 11.2 %all-to-all-done.1 = bf16[8,16,32,128]{3,2,1,0:T(8,128)(2,1)S(1)} async-done(((bf16[8,16,32,128]{3,2,1,0:T(8,128)(2,1)}), bf16[8,16,32,128]{3,2,1,0:T(8,128)(2,1)S(1)}, u32[]{:S(2)}, u32[]{:S(2)}) %all-to-all-start.1) | async-done | bytes 1048608 | tf_op jit(solution)/shard_map/all_to_all | solution.py:106
  83.1 3.6 all-to-all-start.2
  102.9 4.7 %all-to-all-done.2 = bf16[8,16,32,128]{3,2,1,0:T(8,128)(2,1)S(1)} async-done(((bf16[8,16,32,128]{3,2,1,0:T(8,128)(2,1)}), bf16[8,16,32,128]{3,2,1,0:T(8,128)(2,1)S(1)}, u32[]{:S(2)}, u32[]{:S(2)}) %all-to-all-start.2) | async-done | bytes 1048608 | tf_op jit(solution)/shard_map/all_to_all | solution.py:106
  107.5 3.6 all-to-all-start.3
  143.5 49.8 %while.4 = (s32[]{:T(128)}, bf16[512,2,512]{2,1,0:T(2,128)(2,1)}, s32[16,3]{0,1:T(4,128)S(1)}, bf16[16,128,2,128]{1,3,2,0:T(8,128)(2,1)S(1)}, s32[]{:T(128)}) while((s32[]{:T(128)}, bf16[512,2,512]{2,1,0:T(2,128)(2,1)}, s32[16,3]{0,1:T(4,128)S(1)}, bf16[16,128,2,128]{1,3,2,0:T(8,128)(2,1)S(1)}, s32[]{:T(128)}) %tuple.193), condition=%wide.while_cond, body=%wide.while_body.sunk | while | flops 2 | bytes 393333 | solution.py:63
  193.5 51.8 %while.5 = (s32[]{:T(128)}, bf16[512,2,512]{2,1,0:T(2,128)(2,1)}, s32[16,3]{0,1:T(4,128)S(1)}, bf16[16,128,2,128]{1,3,2,0:T(8,128)(2,1)S(1)}, s32[]{:T(128)}) while((s32[]{:T(128)}, bf16[512,2,512]{2,1,0:T(2,128)(2,1)}, s32[16,3]{0,1:T(4,128)S(1)}, bf16[16,128,2,128]{1,3,2,0:T(8,128)(2,1)S(1)}, s32[]{:T(128)}) %tuple.196), condition=%wide.while_cond.1, body=%wide.while_body.1.sunk | while | flops 2 | bytes 393333 | solution.py:63
  194.2 2.4 dynamic-slice_bitcast_fusion.9
  197.5 2.4 dynamic-slice_bitcast_fusion.9
  200.7 2.4 dynamic-slice_bitcast_fusion.9
  203.9 2.4 dynamic-slice_bitcast_fusion.9
  207.2 2.4 dynamic-slice_bitcast_fusion.9
  213.6 2.4 dynamic-slice_bitcast_fusion.9
  216.9 2.4 dynamic-slice_bitcast_fusion.9
  220.1 2.4 dynamic-slice_bitcast_fusion.9
  223.3 2.4 dynamic-slice_bitcast_fusion.9
  226.6 2.4 dynamic-slice_bitcast_fusion.9
  236.3 2.4 dynamic-slice_bitcast_fusion.9
  239.5 2.4 dynamic-slice_bitcast_fusion.9
  245.5 51.8 %while.6 = (s32[]{:T(128)}, bf16[512,2,512]{2,1,0:T(2,128)(2,1)}, s32[16,3]{0,1:T(4,128)S(1)}, bf16[16,128,2,128]{1,3,2,0:T(8,128)(2,1)S(1)}, s32[]{:T(128)}) while((s32[]{:T(128)}, bf16[512,2,512]{2,1,0:T(2,128)(2,1)}, s32[16,3]{0,1:T(4,128)S(1)}, bf16[16,128,2,128]{1,3,2,0:T(8,128)(2,1)S(1)}, s32[]{:T(128)}) %tuple.199), condition=%wide.while_cond.2, body=%wide.while_body.2.sunk | while | flops 2 | bytes 393333 | solution.py:63
  297.6 51.7 %while.7 = (s32[]{:T(128)}, bf16[512,2,512]{2,1,0:T(2,128)(2,1)}, s32[16,3]{0,1:T(4,128)S(1)}, bf16[16,128,2,128]{1,3,2,0:T(8,128)(2,1)S(1)}, s32[]{:T(128)}) while((s32[]{:T(128)}, bf16[512,2,512]{2,1,0:T(2,128)(2,1)}, s32[16,3]{0,1:T(4,128)S(1)}, bf16[16,128,2,128]{1,3,2,0:T(8,128)(2,1)S(1)}, s32[]{:T(128)}) %tuple.202), condition=%wide.while_cond.3, body=%wide.while_body.3.sunk | while | flops 2 | bytes 393333 | solution.py:63
  349.4 2.5 fusion.17
  354.2 2.8 convolution_convert_fusion.3
  357.0 2.8 convert_bitcast_fusion.7
  359.8 2.8 convert_bitcast_fusion.6
  362.6 2.8 convolution_convert_fusion.2
  365.4 2.7 convert_bitcast_fusion.4
  368.1 2.8 convert_bitcast_fusion.5
  370.9 2.8 convolution_convert_fusion.1
  373.8 2.8 convert_bitcast_fusion.2
  376.5 2.8 convert_bitcast_fusion.3
  379.4 2.8 convolution_convert_fusion
  383.8 2.8 convert_bitcast_fusion.1
  386.6 2.4 pad_maximum_fusion
  389.1 3.1 gather_fusion.2
  392.2 10.0 %fusion.16 = f32[16,512,256]{1,2,0:T(8,128)S(1)} fusion(f32[16,512]{1,0:T(8,128)S(1)} %copy-done.27, s32[16,512]{1,0:T(8,128)S(1)} %copy-done.49, f32[16,512]{1,0:T(8,128)S(1)} %copy-done.50, s32[16,512]{1,0:T(8,128)S(1)} %copy-done.25, bf16[16,128,256]{1,2,0:T(8,128)(2,1)S(1)} %gather_fusion.2, pred[16]{0:T(512)(128)(4,1)S(1)} %copy-done.83), kind=kOutput, calls=%fused_computation.112 | convolution fusion | flops 543686656 | bytes 9568272 | tf_op jit(solution)/shard_map/bns,bsk->bnk/dot_general | solution.py:52
  405.3 4.7 %pad_maximum_fusion.1 = bf16[64,128,256]{1,2,0:T(8,128)(2,1)} fusion(bf16[64,128,128]{1,2,0:T(8,128)(2,1)} %convert_bitcast_fusion.4, bf16[64,128,128]{1,2,0:T(8,128)(2,1)} %convert_bitcast_fusion.5), kind=kLoop, calls=%fused_computation.57 | loop fusion | flops 8388608 | bytes 8388608 | tf_op jit(solution)/shard_map/concatenate | solution.py:38
  410.0 3.1 gather_fusion.5
  413.9 2.6 fusion.19
  422.7 4.8 %pad_maximum_fusion.2 = bf16[64,128,256]{1,2,0:T(8,128)(2,1)} fusion(bf16[64,128,128]{1,2,0:T(8,128)(2,1)} %convert_bitcast_fusion.2, bf16[64,128,128]{1,2,0:T(8,128)(2,1)} %convert_bitcast_fusion.3), kind=kLoop, calls=%fused_computation.58 | loop fusion | flops 8388608 | bytes 8388608 | tf_op jit(solution)/shard_map/concatenate | solution.py:38
  427.5 3.1 gather_fusion.8
  431.5 2.6 fusion.21
  440.6 4.1 pad_maximum_fusion.3
  444.7 3.1 gather_fusion.11
  (661 shorter events, 269.1 us)
Async XLA Ops:
  8.0 135.2 %all-reduce.3.cloned.1.call-start = ((), (), s32[]{:S(2)}) async-start(), calls=%async_computation.8 | async-start | bytes 8388608 | tf_op jit(solution)/shard_map/psum | solution.py:11
  20.1 42.4 %copy-start.78 = (s32[8,64]{1,0:T(8,128)}, s32[8,64]{1,0:T(8,128)S(1)}, u32[]{:S(2)}) copy-start(s32[8,64]{1,0:T(8,128)S(1)} %get-tuple-element.85) | copy-start | bytes 6148
  22.8 32.1 %all-to-all-start = ((bf16[8,16,32,128]{3,2,1,0:T(8,128)(2,1)}), bf16[8,16,32,128]{3,2,1,0:T(8,128)(2,1)S(1)}, u32[]{:S(2)}, u32[]{:S(2)}) async-start(bf16[8,16,32,128]{3,2,1,0:T(8,128)(2,1)} %bitcast.5), calls=%async_computation | async-start | bytes 2097152 | tf_op jit(solution)/shard_map/all_to_all | solution.py:106
  28.0 326.2 %all-gather.5.cloned.1.call-start = ((), (), s32[]{:S(2)}) async-start(), calls=%async_computation.4 | async-start | bytes 2621440 | tf_op jit(solution)/shard_map/all_gather | solution.py:142
  57.3 10.2 %copy-start.7 = (f32[4,4,8192]{2,1,0:T(4,128)S(1)}, f32[4,4,8192]{2,1,0:T(4,128)}, u32[]{:S(2)}) copy-start(f32[4,4,8192]{2,1,0:T(4,128)} %param.23) | copy-start | bytes 1572868
  58.4 11.5 %copy-start.84 = (s32[4,16]{1,0:T(4,128)S(1)}, s32[4,16]{1,0:T(4,128)}, u32[]{:S(2)}) copy-start(s32[4,16]{1,0:T(4,128)} %param.19) | copy-start | bytes 772
  58.5 24.6 %all-to-all-start.1 = ((bf16[8,16,32,128]{3,2,1,0:T(8,128)(2,1)}), bf16[8,16,32,128]{3,2,1,0:T(8,128)(2,1)S(1)}, u32[]{:S(2)}, u32[]{:S(2)}) async-start(bf16[8,16,32,128]{3,2,1,0:T(8,128)(2,1)} %bitcast.25), calls=%async_computation.1 | async-start | bytes 2097152 | tf_op jit(solution)/shard_map/all_to_all | solution.py:106
  71.8 17.8 %copy-start.72 = (s32[8192]{0:T(1024)S(1)}, s32[8192]{0:T(1024)}, u32[]{:S(2)}) copy-start(s32[8192]{0:T(1024)} %get-tuple-element.234) | copy-start | bytes 98308
  71.8 17.8 %copy-start.76 = (f32[8192]{0:T(1024)S(1)}, f32[8192]{0:T(1024)}, u32[]{:S(2)}) copy-start(f32[8192]{0:T(1024)} %get-tuple-element.67) | copy-start | bytes 98308
  71.8 17.8 %copy-start.71 = (s32[8192]{0:T(1024)S(1)}, s32[8192]{0:T(1024)}, u32[]{:S(2)}) copy-start(s32[8192]{0:T(1024)} %get-tuple-element.235) | copy-start | bytes 98308
  71.8 17.9 %copy-start.75 = (f32[8192]{0:T(1024)S(1)}, f32[8192]{0:T(1024)}, u32[]{:S(2)}) copy-start(f32[8192]{0:T(1024)} %get-tuple-element.66) | copy-start | bytes 98308
  71.8 17.9 %copy-start.70 = (s32[8192]{0:T(1024)S(1)}, s32[8192]{0:T(1024)}, u32[]{:S(2)}) copy-start(s32[8192]{0:T(1024)} %get-tuple-element.75) | copy-start | bytes 98308
  71.8 17.9 %copy-start.74 = (f32[8192]{0:T(1024)S(1)}, f32[8192]{0:T(1024)}, u32[]{:S(2)}) copy-start(f32[8192]{0:T(1024)} %get-tuple-element.65) | copy-start | bytes 98308
  71.8 17.9 %copy-start.69 = (s32[8192]{0:T(1024)S(1)}, s32[8192]{0:T(1024)}, u32[]{:S(2)}) copy-start(s32[8192]{0:T(1024)} %get-tuple-element.74) | copy-start | bytes 98308
  71.8 18.0 %copy-start.73 = (f32[8192]{0:T(1024)S(1)}, f32[8192]{0:T(1024)}, u32[]{:S(2)}) copy-start(f32[8192]{0:T(1024)} %get-tuple-element.64) | copy-start | bytes 98308
  71.8 18.0 %copy-start.67 = (s32[8192]{0:T(1024)S(1)}, s32[8192]{0:T(1024)}, u32[]{:S(2)}) copy-start(s32[8192]{0:T(1024)} %get-tuple-element.73) | copy-start | bytes 98308
  71.8 18.1 %copy-start.65 = (s32[8192]{0:T(1024)S(1)}, s32[8192]{0:T(1024)}, u32[]{:S(2)}) copy-start(s32[8192]{0:T(1024)} %get-tuple-element.70) | copy-start | bytes 98308
  71.8 18.1 %copy-start.64 = (s32[8192]{0:T(1024)S(1)}, s32[8192]{0:T(1024)}, u32[]{:S(2)}) copy-start(s32[8192]{0:T(1024)} %get-tuple-element.238) | copy-start | bytes 98308
  71.8 18.1 %copy-start.63 = (s32[8192]{0:T(1024)S(1)}, s32[8192]{0:T(1024)}, u32[]{:S(2)}) copy-start(s32[8192]{0:T(1024)} %get-tuple-element.239) | copy-start | bytes 98308
  83.1 24.5 %all-to-all-start.2 = ((bf16[8,16,32,128]{3,2,1,0:T(8,128)(2,1)}), bf16[8,16,32,128]{3,2,1,0:T(8,128)(2,1)S(1)}, u32[]{:S(2)}, u32[]{:S(2)}) async-start(bf16[8,16,32,128]{3,2,1,0:T(8,128)(2,1)} %bitcast.43), calls=%async_computation.2 | async-start | bytes 2097152 | tf_op jit(solution)/shard_map/all_to_all | solution.py:106
  86.6 275.9 %all-gather.7.cloned.1.call-start = ((), (), s32[]{:S(2)}) async-start(), calls=%async_computation.5 | async-start | bytes 2621440 | tf_op jit(solution)/shard_map/all_gather | solution.py:142
  89.5 22.4 %copy-start.24 = (s32[16,512]{1,0:T(8,128)}, s32[16,512]{1,0:T(8,128)S(1)}, u32[]{:S(2)}) copy-start(s32[16,512]{1,0:T(8,128)S(1)} %eq.616) | copy-start | bytes 98308
  89.6 22.4 %copy-start.26 = (f32[16,512]{1,0:T(8,128)}, f32[16,512]{1,0:T(8,128)S(1)}, u32[]{:S(2)}) copy-start(f32[16,512]{1,0:T(8,128)S(1)} %broadcast_in_dim_squeeze.8) | copy-start | bytes 98308
  89.6 22.4 %copy-start.20 = (s32[16,512]{1,0:T(8,128)}, s32[16,512]{1,0:T(8,128)S(1)}, u32[]{:S(2)}) copy-start(s32[16,512]{1,0:T(8,128)S(1)} %eq.632) | copy-start | bytes 98308
  89.6 22.3 %copy-start.22 = (f32[16,512]{1,0:T(8,128)}, f32[16,512]{1,0:T(8,128)S(1)}, u32[]{:S(2)}) copy-start(f32[16,512]{1,0:T(8,128)S(1)} %broadcast_in_dim_squeeze.9) | copy-start | bytes 98308
  89.7 22.3 %copy-start.32 = (s32[16,512]{1,0:T(8,128)}, s32[16,512]{1,0:T(8,128)S(1)}, u32[]{:S(2)}) copy-start(s32[16,512]{1,0:T(8,128)S(1)} %eq.639) | copy-start | bytes 98308
  89.7 22.3 %copy-start.33 = (f32[16,512]{1,0:T(8,128)}, f32[16,512]{1,0:T(8,128)S(1)}, u32[]{:S(2)}) copy-start(f32[16,512]{1,0:T(8,128)S(1)} %broadcast_in_dim_squeeze.10) | copy-start | bytes 98308
  89.7 22.3 %copy-start.28 = (s32[16,512]{1,0:T(8,128)}, s32[16,512]{1,0:T(8,128)S(1)}, u32[]{:S(2)}) copy-start(s32[16,512]{1,0:T(8,128)S(1)} %eq.647) | copy-start | bytes 98308
  89.8 22.2 %copy-start.30 = (f32[16,512]{1,0:T(8,128)}, f32[16,512]{1,0:T(8,128)S(1)}, u32[]{:S(2)}) copy-start(f32[16,512]{1,0:T(8,128)S(1)} %broadcast_in_dim_squeeze.11) | copy-start | bytes 98308
  89.8 24.9 %copy-start.10 = (s32[16,512]{1,0:T(8,128)}, s32[16,512]{1,0:T(8,128)S(1)}, u32[]{:S(2)}) copy-start(s32[16,512]{1,0:T(8,128)S(1)} %eq.676) | copy-start | bytes 98308
  89.8 25.5 %copy-start.8 = (s32[16,512]{1,0:T(8,128)}, s32[16,512]{1,0:T(8,128)S(1)}, u32[]{:S(2)}) copy-start(s32[16,512]{1,0:T(8,128)S(1)} %eq.684) | copy-start | bytes 98308
  100.4 37.2 %copy-start.58 = (s32[8192]{0:T(1024)S(1)}, s32[8192]{0:T(1024)}, u32[]{:S(2)}) copy-start(s32[8192]{0:T(1024)} %get-tuple-element.233) | copy-start | bytes 98308
  101.0 36.6 %copy-start.57 = (s32[8192]{0:T(1024)S(1)}, s32[8192]{0:T(1024)}, u32[]{:S(2)}) copy-start(s32[8192]{0:T(1024)} %get-tuple-element.240) | copy-start | bytes 98308
  107.5 32.5 %all-to-all-start.3 = ((bf16[8,16,32,128]{3,2,1,0:T(8,128)(2,1)}), bf16[8,16,32,128]{3,2,1,0:T(8,128)(2,1)S(1)}, u32[]{:S(2)}, u32[]{:S(2)}) async-start(bf16[8,16,32,128]{3,2,1,0:T(8,128)(2,1)} %bitcast.61), calls=%async_computation.3 | async-start | bytes 2097152 | tf_op jit(solution)/shard_map/all_to_all | solution.py:106
  111.1 259.8 %all-gather.9.cloned.1.call-start = ((), (), s32[]{:S(2)}) async-start(), calls=%async_computation.6 | async-start | bytes 2621440 | tf_op jit(solution)/shard_map/all_gather | solution.py:142
  113.7 265.7 %all-gather.11.cloned.1.call-start = ((), (), s32[]{:S(2)}) async-start(), calls=%async_computation.7 | async-start | bytes 2621440 | tf_op jit(solution)/shard_map/all_gather | solution.py:142
  245.3 52.1 %copy-start.4 = (bf16[16,128,2,128]{1,3,2,0:T(8,128)(2,1)}, bf16[16,128,2,128]{1,3,2,0:T(8,128)(2,1)S(1)}, u32[]{:S(2)}) copy-start(bf16[16,128,2,128]{1,3,2,0:T(8,128)(2,1)S(1)} %get-tuple-element.20) | copy-start | bytes 3145732
  297.3 54.5 %copy-start.5 = (bf16[16,128,2,128]{1,3,2,0:T(8,128)(2,1)}, bf16[16,128,2,128]{1,3,2,0:T(8,128)(2,1)S(1)}, u32[]{:S(2)}) copy-start(bf16[16,128,2,128]{1,3,2,0:T(8,128)(2,1)S(1)} %get-tuple-element.28) | copy-start | bytes 3145732
  392.2 10.0 %copy-start.21 = (s32[16,512]{1,0:T(8,128)S(1)}, s32[16,512]{1,0:T(8,128)}, u32[]{:S(2)}) copy-start(s32[16,512]{1,0:T(8,128)} %copy-done.20) | copy-start | bytes 98308
  392.2 10.0 %copy-start.23 = (f32[16,512]{1,0:T(8,128)S(1)}, f32[16,512]{1,0:T(8,128)}, u32[]{:S(2)}) copy-start(f32[16,512]{1,0:T(8,128)} %copy-done.22) | copy-start | bytes 98308
  392.2 10.0 %copy-start.46 = (s32[16,512]{1,0:T(8,128)S(1)}, s32[16,512]{1,0:T(8,128)}, u32[]{:S(2)}) copy-start(s32[16,512]{1,0:T(8,128)} %broadcast_add_fusion.14) | copy-start | bytes 98308
  392.2 10.0 %copy-start.47 = (f32[16,512]{1,0:T(8,128)S(1)}, f32[16,512]{1,0:T(8,128)}, u32[]{:S(2)}) copy-start(f32[16,512]{1,0:T(8,128)} %broadcast_subtract_fusion.14) | copy-start | bytes 98308
  405.3 8.6 %copy-start.11 = (s32[16,512]{1,0:T(8,128)S(1)}, s32[16,512]{1,0:T(8,128)}, u32[]{:S(2)}) copy-start(s32[16,512]{1,0:T(8,128)} %copy-done.10) | copy-start | bytes 98308
  422.7 7.9 %copy-start.55 = (f32[16,512]{1,0:T(8,128)S(1)}, f32[16,512]{1,0:T(8,128)}, u32[]{:S(2)}) copy-start(f32[16,512]{1,0:T(8,128)} %squeeze.179) | copy-start | bytes 98308
  422.7 8.7 %copy-start.43 = (s32[16,512]{1,0:T(8,128)S(1)}, s32[16,512]{1,0:T(8,128)}, u32[]{:S(2)}) copy-start(s32[16,512]{1,0:T(8,128)} %broadcast_add_fusion.5) | copy-start | bytes 98308
  440.6 8.1 %copy-start.3 = (bf16[16,128,2,128]{1,3,2,0:T(8,128)(2,1)S(1)}, bf16[16,128,2,128]{1,3,2,0:T(8,128)(2,1)}, u32[]{:S(2)}) copy-start(bf16[16,128,2,128]{1,3,2,0:T(8,128)(2,1)} %copy-done.2) | copy-start | bytes 3145732
  440.6 8.1 %copy-start.19 = (s32[16,512]{1,0:T(8,128)S(1)}, s32[16,512]{1,0:T(8,128)}, u32[]{:S(2)}) copy-start(s32[16,512]{1,0:T(8,128)} %copy-done.18) | copy-start | bytes 98308
  440.6 8.1 %copy-start.40 = (s32[16,512]{1,0:T(8,128)S(1)}, s32[16,512]{1,0:T(8,128)}, u32[]{:S(2)}) copy-start(s32[16,512]{1,0:T(8,128)} %broadcast_add_fusion.1) | copy-start | bytes 98308
  (46 other events, 140.2 us)
Sparse Core Ops, SparseCore 0:
  18.4 124.7 all-reduce.2
Sparse Core Ops, SparseCore 1:
  56.6 44.9 all-gather.4
  103.1 44.3 all-gather.6
  149.0 44.3 all-gather.8
  195.0 44.4 all-gather.10
where the time goes:
time: 473 us; the launch traced here: 465 us
  local copies, waits for them, and re-layouts  252 us (53%)
  other arithmetic  73.5 us (16%)
  matrix products  56 us (12%)
  waiting for transfers between devices  44.3 us (9%)
  between operations  20.4 us (4%)
  starting transfers between devices  16.4 us (3%)
    gather x320, local copies, waits for them, and re-layouts  203 us
    all_to_all x4, waiting for transfers between devices, fetch_strips(): lax.all_to_all(outgoing, 'rays', split_axis=0, concat_axis=0, tiled=True)  42.7 us
    dot_general x8, matrix products, interpolate(): jnp.einsum('bns,bsk->bnk', row_weight.astype(jnp.bfloat16), lookup, prefe...  23.7 us
    concatenate x4, other arithmetic, convolve(): jnp.concatenate([along_rows, along_cols], axis=2).astype(jnp.bfloat16)  16.1 us
    all_to_all x4, starting transfers between devices, fetch_strips(): lax.all_to_all(outgoing, 'rays', split_axis=0, concat_axis=0, tiled=True)  16 us
    reduce_sum x8, other arithmetic, interpolate(): along_x = jnp.sum(row_values[..., :side] * col_weight, axis=-1)  14 us
    gather x4, local copies, waits for them, and re-layouts, per_device(): fine_lookup = jnp.take(fields, block_slots[plane_index], axis=0)  12.2 us
    dot_general x4, matrix products, convolve(): jnp.einsum('lij,jk->lik', density, right_table, preferred_element_type=jn...  11.3 us
  transfers between devices with their start and end apart: 9, of which 4 were waited for; matrix products, arithmetic and copies ran while one was open for 64% of the time, Pallas kernels for 0%

commit v1 on v0

v1 whole, which is shorter than its diff:
```python
import functools

import jax
import jax.numpy as jnp
import numpy as np
from jax import lax
from jax.experimental import pallas as pl
from jax.experimental.pallas import tpu as pltpu
from jax.sharding import PartitionSpec as P

RATIO = 16
ROW_ALIGN = 16
COL_ALIGN = 128


def kernel_tables(side):
    indices = np.arange(side)
    offset = (indices[:, None] - indices[None, :]).astype(np.float32)
    taps = np.arange(-6, 7).astype(np.float32)
    total = np.sum(np.exp(-taps * taps / np.float32(8.0)))
    inside = np.abs(offset) <= 6.0
    weight = np.where(inside, np.exp(-offset * offset / np.float32(8.0)), np.float32(0.0)) / total
    smooth = weight.astype(jnp.bfloat16)
    slope = (np.float32(6.0) * offset * weight / np.float32(4.0)).astype(jnp.bfloat16)
    return np.concatenate([smooth, slope], axis=0)


def dot_nt(a, b):
    return lax.dot_general(a, b, (((1,), (1,)), ((), ())), preferred_element_type=jnp.float32)


def hat(positions, cell, frac):
    return jnp.where(
        positions == cell, 1.0 - frac, jnp.where(positions == cell + 1, frac, 0.0)
    )


def look_up(table, row_cell, col_cell, row_frac, col_frac):
    side = table.shape[0] // 2
    width = row_cell.shape[1]
    rows = lax.broadcasted_iota(jnp.int32, (table.shape[1], width), 0)
    cols = lax.broadcasted_iota(jnp.int32, (side, width), 0)
    row_weight = hat(rows, row_cell, row_frac).astype(jnp.bfloat16)
    col_weight = hat(cols, col_cell, col_frac)
    values = jnp.dot(table, row_weight, preferred_element_type=jnp.float32)
    along_x = jnp.sum(values[:side] * col_weight, axis=0, keepdims=True)
    along_y = jnp.sum(values[side:] * col_weight, axis=0, keepdims=True)
    return along_x, along_y


def tile_fields(tile, tables):
    side = tile.shape[0]
    part = dot_nt(tables, tile).astype(jnp.bfloat16)
    along_x = dot_nt(part[:side], tables[side:])
    along_y = dot_nt(part[side:], tables[:side])
    return jnp.concatenate([along_x, along_y], axis=0).astype(jnp.bfloat16)


def map_window(read, row_start, col_start, side, map_side):
    rows = min(side + ROW_ALIGN, map_side)
    cols = min(side + COL_ALIGN, map_side)
    row_base = jnp.minimum(row_start // ROW_ALIGN * ROW_ALIGN, map_side - rows)
    col_base = jnp.minimum(col_start // COL_ALIGN * COL_ALIGN, map_side - cols)
    row_base = pl.multiple_of(row_base, ROW_ALIGN)
    col_base = pl.multiple_of(col_base, COL_ALIGN)
    here = lax.broadcasted_iota(jnp.int32, (side, cols), 0)
    there = lax.broadcasted_iota(jnp.int32, (side, cols), 1)
    pick = (there == here + (col_start - col_base)).astype(jnp.float32).astype(jnp.bfloat16)
    along_x = dot_nt(pick, read(0, pl.ds(row_base, rows), pl.ds(col_base, cols)))
    along_y = dot_nt(pick, read(1, pl.ds(row_base, rows), pl.ds(col_base, cols)))
    table = jnp.concatenate([along_x, along_y], axis=0).astype(jnp.bfloat16)
    return table, row_start - row_base


def plane_kernel(plane, last, windows, tables, strips, used, fine, long, fractions, *rest):
    previous, outs = rest[:plane], rest[plane:]
    block = pl.program_id(0)
    side = strips.shape[2]
    tile = strips[...].reshape(side, side)
    fields = tile_fields(tile, tables[...])
    window, row_extra = map_window(
        lambda c, r, s: used[c, r, s],
        windows[0, block],
        windows[1, block],
        side,
        used.shape[1],
    )
    shift_x = jnp.zeros_like(fractions[0:1, :])
    shift_y = shift_x
    for j, earlier in enumerate(previous):
        shift_x = shift_x - ((plane - j) / plane) * earlier[0:1, :]
        shift_y = shift_y - ((plane - j) / plane) * earlier[1:2, :]
    fine_x, fine_y = look_up(
        fields,
        fine[0:1, :],
        fine[1:2, :],
        fractions[0:1, :] + shift_x,
        fractions[1:2, :] + shift_y,
    )
    long_x, long_y = look_up(
        window,
        long[0:1, :] + row_extra,
        long[1:2, :],
        fractions[2:3, :] + shift_x / RATIO,
        fractions[3:4, :] + shift_y / RATIO,
    )
    value = jnp.concatenate([fine_x + long_x, fine_y + long_y], axis=0)
    outs[0][...] = value
    if last:
        count = plane + 1
        source = jnp.zeros_like(value)
        for j, earlier in enumerate(previous):
            source = source - ((count - j) / count) * earlier[...]
        outs[1][...] = source - (1 / count) * value


def run_plane(plane, last, windows, tables, strips, used, fine, long, fractions, previous):
    blocks = windows.shape[1]
    rays_here = fine.shape[1]
    width = rays_here // blocks
    rows = lambda n: pl.BlockSpec((n, width), lambda b: (0, b))
    whole = lambda x: pl.BlockSpec(x.shape, lambda b: (0,) * x.ndim)
    shape = jax.ShapeDtypeStruct((2, rays_here), jnp.float32)
    out_count = 2 if last else 1
    return pl.pallas_call(
        functools.partial(plane_kernel, plane, last),
        grid=(blocks,),
        out_shape=[shape] * out_count,
        in_specs=[
            pl.BlockSpec(memory_space=pltpu.SMEM),
            whole(tables),
            pl.BlockSpec((strips.shape[0], None, strips.shape[2], strips.shape[3]), lambda b: (0, b, 0, 0)),
            whole(used),
            rows(2),
            rows(2),
            rows(4),
        ]
        + [rows(2)] * plane,
        out_specs=[rows(2)] * out_count,
        compiler_params=pltpu.CompilerParams(vmem_limit_bytes=40 * 1024 * 1024),
        cost_estimate=pl.CostEstimate(
            flops=6 * rays_here * 128 * 256, bytes_accessed=4 << 20, transcendentals=0
        ),
    )(windows, tables, strips, used, fine, long, fractions, *previous)


def per_device(
    tile_density,
    long_maps,
    map_owner,
    tile_lists,
    block_slots,
    block_windows,
    fine_cells,
    long_cells,
    fractions,
):
    my_row = lax.axis_index("rays")
    strip_count = lax.axis_size("planes")
    plane_count, _, _, side = tile_density.shape
    tables = jnp.asarray(kernel_tables(side))
    blocks = block_slots.shape[1]

    slots = lax.all_gather(block_slots, "planes", axis=0)
    lists = lax.dynamic_index_in_dim(tile_lists, my_row, 0, keepdims=False)
    wanted = jnp.take_along_axis(lists[None], slots, axis=2)
    mine = (map_owner == my_row)[:, None, None, None]

    deflection = []
    for plane in range(plane_count):
        every = lax.all_gather(tile_density[plane], "rays", axis=0, tiled=True)
        out = jnp.take(every, wanted[:, plane].reshape(-1), axis=0, mode="clip")
        out = out.reshape((strip_count, blocks) + every.shape[1:])
        strips = lax.all_to_all(out, "planes", split_axis=0, concat_axis=0, tiled=True)
        own = jnp.transpose(long_maps[0, plane], (1, 0, 2))
        used = lax.psum(jnp.where(mine[plane], own, jnp.zeros_like(own)), "rays")
        result = run_plane(
            plane,
            plane == plane_count - 1,
            block_windows[plane],
            tables,
            strips,
            used,
            fine_cells[plane],
            long_cells[plane],
            fractions[plane],
            deflection,
        )
        deflection.append(result[0])
    return jnp.stack(deflection), result[1]


def solution(mesh):
    return jax.shard_map(
        per_device,
        mesh=mesh,
        in_specs=(
            P(None, "rays", "planes", None),
            P("rays", None, None, None, None),
            P(),
            P(),
            P(None, ("rays", "planes")),
            P(None, None, ("rays", "planes")),
            P(None, None, ("rays", "planes")),
            P(None, None, ("rays", "planes")),
            P(None, None, ("rays", "planes")),
        ),
        out_specs=(P(None, None, ("rays", "planes")), P(None, ("rays", "planes"))),
        check_vma=False,
    )
```

time: 473 us -> 267 us (0.56); the launches traced: 465 us -> 266 us
  local copies, waits for them, and re-layouts: 252 us -> 25.9 us
  waiting for transfers between devices: 44.3 us -> 144 us
  other arithmetic: 73.5 us -> 8.14 us
  matrix products: 56 us -> 0 us
  Pallas kernels: 0 us -> 42.4 us
  blocking collectives: 0 us -> 13.5 us
  between operations: 20.4 us -> 14 us
    gather x332 -> x7, local copies, waits for them, and re-layouts: 221 us -> 14.8 us  [the longest x4 12.2 us: per_device(): out = jnp.take(every, wanted[:, plane].reshape(-1), axis=0, mode='clip')]
    psum x1, waiting for transfers between devices: 1.52 us -> 76.2 us  [per_device(): used = lax.psum(jnp.where(mine[plane], own, jnp.zeros_like(own)), 'rays')]
    all_gather x4, waiting for transfers between devices: 0.01 us -> 65.8 us  [per_device(): every = lax.all_gather(tile_density[plane], 'rays', axis=0, tiled=True)]
    dot_general x20 -> x0, matrix products: 56 us -> none  [the longest x8 23.7 us: interpolate(): jnp.einsum('bns,bsk->bnk', row_weight.astype(jnp.bfloat16), lookup, prefe...]
    all_to_all x4, waiting for transfers between devices: 42.7 us -> 0.01 us  [per_device(): lax.all_to_all(out, 'planes', split_axis=0, concat_axis=0, tiled=True)]
    pallas_call x0 -> x4, Pallas kernels: none -> 42.4 us  [run_plane(): pl.pallas_call(functools.partial(plane_kernel, plane, last), grid=(blocks...]
    reduce_sum x14 -> x0, other arithmetic: 16.4 us -> none  [the longest x8 14 us: interpolate(): along_x = jnp.sum(row_values[..., :side] * col_weight, axis=-1)]
    concatenate x5 -> x0, other arithmetic: 16.1 us -> none  [the longest x4 16.1 us: convolve(): jnp.concatenate([along_rows, along_cols], axis=2).astype(jnp.bfloat16)]
  transfers between devices with their start and end apart: 9 -> 9, of which waited for: 4 -> 5; matrix products, arithmetic and copies ran while one was open for 64% -> 11% of each run, Pallas kernels for 0% -> 12%
where the time goes in v1:
time: 267 us; the launch traced here: 266 us
  waiting for transfers between devices  144 us (54%)
  Pallas kernels  42.4 us (16%)
  local copies, waits for them, and re-layouts  25.9 us (10%)
  starting transfers between devices  18.6 us (7%)
  between operations  14 us (5%)
  blocking collectives  13.5 us (5%)
  other arithmetic  8.14 us (3%)
    psum x1, waiting for transfers between devices, per_device(): used = lax.psum(jnp.where(mine[plane], own, jnp.zeros_like(own)), 'rays')  76.2 us
    all_gather x4, waiting for transfers between devices, per_device(): every = lax.all_gather(tile_density[plane], 'rays', axis=0, tiled=True)  65.8 us
    pallas_call x4, Pallas kernels, run_plane(): pl.pallas_call(functools.partial(plane_kernel, plane, last), grid=(blocks...  42.4 us
    all_to_all x4, starting transfers between devices, per_device(): lax.all_to_all(out, 'planes', split_axis=0, concat_axis=0, tiled=True)  18.4 us
    all_gather x1, blocking collectives, per_device(): slots = lax.all_gather(block_slots, 'planes', axis=0)  13.5 us
    gather x4, local copies, waits for them, and re-layouts, per_device(): out = jnp.take(every, wanted[:, plane].reshape(-1), axis=0, mode='clip')  12.2 us
    select_n x2, other arithmetic, per_device(): used = lax.psum(jnp.where(mine[plane], own, jnp.zeros_like(own)), 'rays')  7.27 us
    slice x1, local copies, waits for them, and re-layouts, per_device(): own = jnp.transpose(long_maps[0, plane], (1, 0, 2))  5.55 us
  transfers between devices with their start and end apart: 9, of which 5 were waited for; matrix products, arithmetic and copies ran while one was open for 11% of the time, Pallas kernels for 12%

profile of v1, /device:TPU:0, one launch (start us, length us, event | category | flops | bytes accessed | tf_op | source)
XLA Modules:
  0.0 266.5 jit_solution(10155371295287066329)
XLA Ops:
  7.2 0.0 copy-start
  7.2 0.0 all-gather.11.cloned.1.call-start
  7.2 2.2 slice_bitcast_fusion.1
  9.4 0.0 all-gather.11.cloned.1.call-update
  9.4 0.0 all-gather.13.cloned.1.call-start
  9.5 0.7 all-gather.13.cloned.1.call-update
  10.2 0.0 all-gather.15.cloned.1.call-start
  10.2 0.7 all-gather.15.cloned.1.call-update
  10.9 0.0 all-gather.17.cloned.1.call-start
  11.0 0.5 all-gather.17.cloned.1.call-update
  11.5 13.5 %all-gather.5 = s32[4,4,16]{2,1,0:T(4,128)S(1)} all-gather(s32[1,4,16]{2,1,0:T(4,128)S(1)} %bitcast.88), channel_id=3, replica_groups=mesh['rays'=8,'planes'=4] {'planes'}, dimensions={0}, use_global_device_ids=true | all-gather | bytes 1280 | tf_op jit(solution)/shard_map/all_gather | solution.py:164
  25.1 0.1 reshape.90
  25.2 2.4 gather_fusion.4
  27.6 0.0 copy-start.9
  27.6 0.1 reshape.93
  27.8 0.1 reshape.60
  27.8 0.1 reshape.68
  27.9 12.6 %all-gather.11.cloned.1.call-done = bf16[1,256,32,128]{3,2,0,1:T(8,128)(2,1)} async-done(((bf16[1,32,32,128]{3,2,0,1:T(8,128)(2,1)}), bf16[1,256,32,128]{3,2,0,1:T(8,128)(2,1)}) %all-gather.11.cloned.1.call-update) | async-done | bytes 2097168 | tf_op jit(solution)/shard_map/all_gather | solution.py:171
  40.5 3.1 %gather_fusion = bf16[64,32,128]{2,1,0:T(8,128)(2,1)} fusion(bf16[256,32,128]{2,1,0:T(8,128)(2,1)} %bitcast.87, s32[1024]{0:T(1024)S(1)} %pad_clamp_fusion.3), kind=kCustom, calls=%fused_computation | custom fusion | bytes 1048832 | tf_op jit(solution)/shard_map/jit(_take)/gather | solution.py:172
  43.6 4.6 %all-to-all-start = ((bf16[4,16,32,128]{3,2,1,0:T(8,128)(2,1)}), bf16[4,16,32,128]{3,2,1,0:T(8,128)(2,1)S(1)}, u32[]{:S(2)}, u32[]{:S(2)}) async-start(bf16[4,16,32,128]{3,2,1,0:T(8,128)(2,1)} %bitcast.5), calls=%async_computation | async-start | bytes 1048576 | tf_op jit(solution)/shard_map/all_to_all | solution.py:174
  48.3 5.5 %fusion.4 = (bf16[1,1,512,2,512]{4,3,2,1,0:T(2,128)(2,1)S(1)}, bf16[1,1,512,2,512]{4,3,2,1,0:T(2,128)(2,1)}, bf16[1,1,512,2,512]{4,3,2,1,0:T(2,128)(2,1)}, bf16[1,1,512,2,512]{4,3,2,1,0:T(2,128)(2,1)S(1)}) fusion(bf16[1,4,512,2,512]{4,3,2,1,0:T(2,128)(2,1)} %param.11), kind=kLoop, calls=%fused_computation.47 | loop fusion | bytes 8388608 | tf_op jit(solution)/shard_map/slice | solution.py:175
  53.8 16.5 %all-gather.13.cloned.1.call-done = bf16[1,256,32,128]{3,2,0,1:T(8,128)(2,1)} async-done(((bf16[1,32,32,128]{3,2,0,1:T(8,128)(2,1)}), bf16[1,256,32,128]{3,2,0,1:T(8,128)(2,1)}) %all-gather.13.cloned.1.call-update) | async-done | bytes 2097168 | tf_op jit(solution)/shard_map/all_gather | solution.py:171
  70.4 3.1 %gather_fusion.1 = bf16[64,32,128]{2,1,0:T(8,128)(2,1)} fusion(bf16[256,32,128]{2,1,0:T(8,128)(2,1)} %bitcast.86, s32[1024]{0:T(1024)S(1)} %pad_clamp_fusion.2), kind=kCustom, calls=%fused_computation.1 | custom fusion | bytes 1048832 | tf_op jit(solution)/shard_map/jit(_take)/gather | solution.py:172
  73.4 4.6 %all-to-all-start.1 = ((bf16[4,16,32,128]{3,2,1,0:T(8,128)(2,1)}), bf16[4,16,32,128]{3,2,1,0:T(8,128)(2,1)S(1)}, u32[]{:S(2)}, u32[]{:S(2)}) async-start(bf16[4,16,32,128]{3,2,1,0:T(8,128)(2,1)} %bitcast.83), calls=%async_computation.1 | async-start | bytes 1048576 | tf_op jit(solution)/shard_map/all_to_all | solution.py:174
  78.0 0.6 fusion.5
  78.6 4.4 %fusion.2 = (bf16[2,512,512]{2,1,0:T(8,128)(2,1)}, bf16[2,512,512]{2,1,0:T(8,128)(2,1)}) fusion(bf16[1,1,512,2,512]{4,3,2,1,0:T(2,128)(2,1)} %get-tuple-element.15, pred[]{:T(512)} %bitcast.16, bf16[1,1,512,2,512]{4,3,2,1,0:T(2,128)(2,1)} %get-tuple-element.16, pred[]{:T(512)} %bitcast.6), kind=kLoop, calls=%fused_computation.10 | loop fusion | flops 1048576 | bytes 4194306 | tf_op jit(solution)/shard_map/jit(_where)/select_n | solution.py:176
  83.0 2.9 %fusion = (bf16[2,512,512]{2,1,0:T(8,128)(2,1)}, bf16[2,512,512]{2,1,0:T(8,128)(2,1)}) fusion(bf16[1,1,512,2,512]{4,3,2,1,0:T(2,128)(2,1)S(1)} %get-tuple-element.17, pred[]{:T(512)} %bitcast.36, bf16[1,1,512,2,512]{4,3,2,1,0:T(2,128)(2,1)S(1)} %get-tuple-element.14, pred[]{:T(512)} %bitcast.26), kind=kLoop, calls=%fused_computation.6 | loop fusion | flops 1048576 | bytes 4194306 | tf_op jit(solution)/shard_map/jit(_where)/select_n | solution.py:176
  85.9 0.0 all-reduce.3.cloned.1.call-update
  85.9 0.0 copy-start.6
  85.9 0.1 reshape.76
  86.0 14.7 %all-gather.15.cloned.1.call-done = bf16[1,256,32,128]{3,2,0,1:T(8,128)(2,1)} async-done(((bf16[1,32,32,128]{3,2,0,1:T(8,128)(2,1)}), bf16[1,256,32,128]{3,2,0,1:T(8,128)(2,1)}) %all-gather.15.cloned.1.call-update) | async-done | bytes 2097168 | tf_op jit(solution)/shard_map/all_gather | solution.py:171
  100.8 3.0 %gather_fusion.2 = bf16[64,32,128]{2,1,0:T(8,128)(2,1)} fusion(bf16[256,32,128]{2,1,0:T(8,128)(2,1)} %bitcast.85, s32[1024]{0:T(1024)S(1)} %pad_clamp_fusion.1), kind=kCustom, calls=%fused_computation.2 | custom fusion | bytes 1048832 | tf_op jit(solution)/shard_map/jit(_take)/gather | solution.py:172
  103.8 0.0 all-to-all-done.1.strips
  103.8 4.6 %all-to-all-start.2 = ((bf16[4,16,32,128]{3,2,1,0:T(8,128)(2,1)}), bf16[4,16,32,128]{3,2,1,0:T(8,128)(2,1)S(1)}, u32[]{:S(2)}, u32[]{:S(2)}) async-start(bf16[4,16,32,128]{3,2,1,0:T(8,128)(2,1)} %bitcast.25), calls=%async_computation.2 | async-start | bytes 1048576 | tf_op jit(solution)/shard_map/all_to_all | solution.py:174
  108.4 0.1 reshape.84
  108.5 21.9 %all-gather.17.cloned.1.call-done = bf16[1,256,32,128]{3,2,0,1:T(8,128)(2,1)} async-done(((bf16[1,32,32,128]{3,2,0,1:T(8,128)(2,1)}), bf16[1,256,32,128]{3,2,0,1:T(8,128)(2,1)}) %all-gather.17.cloned.1.call-update) | async-done | bytes 2097168 | tf_op jit(solution)/shard_map/all_gather | solution.py:171
  130.4 3.0 %gather_fusion.3 = bf16[64,32,128]{2,1,0:T(8,128)(2,1)} fusion(bf16[256,32,128]{2,1,0:T(8,128)(2,1)} %bitcast.84, s32[1024]{0:T(1024)S(1)} %pad_clamp_fusion), kind=kCustom, calls=%fused_computation.3 | custom fusion | bytes 1048832 | tf_op jit(solution)/shard_map/jit(_take)/gather | solution.py:172
  133.5 0.0 all-to-all-done.2.strips
  133.5 4.6 %all-to-all-start.3 = ((bf16[4,16,32,128]{3,2,1,0:T(8,128)(2,1)}), bf16[4,16,32,128]{3,2,1,0:T(8,128)(2,1)S(1)}, u32[]{:S(2)}, u32[]{:S(2)}) async-start(bf16[4,16,32,128]{3,2,1,0:T(8,128)(2,1)} %bitcast.35), calls=%async_computation.3 | async-start | bytes 1048576 | tf_op jit(solution)/shard_map/all_to_all | solution.py:174
  138.1 1.1 slice_bitcast_fusion.10
  139.2 76.2 %all-reduce.3.cloned.1.call-done = (bf16[2,512,512]{2,1,0:T(8,128)(2,1)}, bf16[2,512,512]{2,1,0:T(8,128)(2,1)}, bf16[2,512,512]{2,1,0:T(8,128)(2,1)}, bf16[2,512,512]{2,1,0:T(8,128)(2,1)}) async-done(((bf16[2,512,512]{2,1,0:T(8,128)(2,1)}, bf16[2,512,512]{2,1,0:T(8,128)(2,1)}, bf16[2,512,512]{2,1,0:T(8,128)(2,1)}, bf16[2,512,512]{2,1,0:T(8,128)(2,1)}), (bf16[2,512,512]{2,1,0:T(8,128)(2,1)}, ...) | async-done | bytes 4194320 | tf_op jit(solution)/shard_map/psum | solution.py:176
  215.4 1.2 copy-done.4
  216.6 10.5 %shard_map.113.rest_0_ = f32[2,8192]{1,0:T(2,128)S(1)} custom-call(s32[2,16]{1,0:T(2,128)S(1)} %get-tuple-element.36.windows, bf16[256,128]{1,0:T(8,128)(2,1)S(1)} %copy-done.5, bf16[4,16,32,128]{3,2,1,0:T(8,128)(2,1)S(1)} %all-to-all-done.strips, bf16[2,512,512]{2,1,0:T(8,128)(2,1)S(1)} %copy-done.4, s32[2,8192]{1,0:T(2,128)S(1)} %get-tuple-element.47.fine, ...), custom_call_target="tpu_custom_call" | custom-call | flops 1610612736 | bytes 4194304 | tf_op jit(solution)/shard_map/pallas_call | solution.py:125
  227.1 10.4 %shard_map.114.rest_1_ = f32[2,8192]{1,0:T(2,128)S(1)} custom-call(s32[2,16]{1,0:T(2,128)S(1)} %get-tuple-element.35.windows, bf16[256,128]{1,0:T(8,128)(2,1)S(1)} %copy-done.5, bf16[4,16,32,128]{3,2,1,0:T(8,128)(2,1)S(1)} %all-to-all-done.1.strips, bf16[2,512,512]{2,1,0:T(8,128)(2,1)S(1)} %copy-done.3, s32[2,8192]{1,0:T(2,128)S(1)} %get-tuple-element.48.fine, ...), custom_call_target="tpu_custom_call" | custom-call | flops 1610612736 | bytes 4194304 | tf_op jit(solution)/shard_map/pallas_call | solution.py:125
  237.5 10.4 %shard_map.115.rest_2_ = f32[2,8192]{1,0:T(2,128)S(1)} custom-call(s32[2,16]{1,0:T(2,128)S(1)} %get-tuple-element.34.windows, bf16[256,128]{1,0:T(8,128)(2,1)S(1)} %copy-done.5, bf16[4,16,32,128]{3,2,1,0:T(8,128)(2,1)S(1)} %all-to-all-done.2.strips, bf16[2,512,512]{2,1,0:T(8,128)(2,1)S(1)} %copy-done.2, s32[2,8192]{1,0:T(2,128)S(1)} %get-tuple-element.49.fine, ...), custom_call_target="tpu_custom_call" | custom-call | flops 1610612736 | bytes 4194304 | tf_op jit(solution)/shard_map/pallas_call | solution.py:125
  248.0 0.0 all-to-all-done.3.strips
  248.0 11.1 %shard_map.116 = (f32[2,8192]{1,0:T(2,128)S(1)}, f32[2,8192]{1,0:T(2,128)}) custom-call(s32[2,16]{1,0:T(2,128)S(1)} %get-tuple-element.37.windows, bf16[256,128]{1,0:T(8,128)(2,1)S(1)} %copy-done.5, bf16[4,16,32,128]{3,2,1,0:T(8,128)(2,1)S(1)} %all-to-all-done.3.strips, bf16[2,512,512]{2,1,0:T(8,128)(2,1)S(1)} %copy-done.1, ...), custom_call_target="tpu_custom_call" | custom-call | flops 1610612736 | bytes 4194304 | tf_op jit(solution)/shard_map/pallas_call | solution.py:125
  259.1 0.8 pad_maximum_fusion
  (29 shorter events, 0.2 us)
Async XLA Ops:
  7.2 18.0 %copy-start = (s32[8,4,64]{2,1,0:T(4,128)S(1)}, s32[8,4,64]{2,1,0:T(4,128)}, u32[]{:S(2)}) copy-start(s32[8,4,64]{2,1,0:T(4,128)} %param.13) | copy-start | bytes 24580
  7.2 4.3 %copy-start.8 = (s32[4,16]{1,0:T(4,128)S(1)}, s32[4,16]{1,0:T(4,128)}, u32[]{:S(2)}) copy-start(s32[4,16]{1,0:T(4,128)} %param.14) | copy-start | bytes 772
  7.2 33.4 %all-gather.11.cloned.1.call-start = ((), (), s32[]{:S(2)}) async-start(), calls=%async_computation.4 | async-start | bytes 2359296 | tf_op jit(solution)/shard_map/all_gather | solution.py:171
  9.4 60.9 %all-gather.13.cloned.1.call-start = ((), (), s32[]{:S(2)}) async-start(), calls=%async_computation.5 | async-start | bytes 2359296 | tf_op jit(solution)/shard_map/all_gather | solution.py:171
  10.2 90.6 %all-gather.15.cloned.1.call-start = ((), (), s32[]{:S(2)}) async-start(), calls=%async_computation.6 | async-start | bytes 2359296 | tf_op jit(solution)/shard_map/all_gather | solution.py:171
  10.9 119.5 %all-gather.17.cloned.1.call-start = ((), (), s32[]{:S(2)}) async-start(), calls=%async_computation.7 | async-start | bytes 2359296 | tf_op jit(solution)/shard_map/all_gather | solution.py:171
  27.6 20.6 %copy-start.9 = (s32[4]{0:T(128)S(1)}, s32[4]{0:T(128)}, u32[]{:S(2)}) copy-start(s32[4]{0:T(128)} %param.12) | copy-start | bytes 52
  43.6 29.8 %all-to-all-start = ((bf16[4,16,32,128]{3,2,1,0:T(8,128)(2,1)}), bf16[4,16,32,128]{3,2,1,0:T(8,128)(2,1)S(1)}, u32[]{:S(2)}, u32[]{:S(2)}) async-start(bf16[4,16,32,128]{3,2,1,0:T(8,128)(2,1)} %bitcast.5), calls=%async_computation | async-start | bytes 1048576 | tf_op jit(solution)/shard_map/all_to_all | solution.py:174
  73.4 30.3 %all-to-all-start.1 = ((bf16[4,16,32,128]{3,2,1,0:T(8,128)(2,1)}), bf16[4,16,32,128]{3,2,1,0:T(8,128)(2,1)S(1)}, u32[]{:S(2)}, u32[]{:S(2)}) async-start(bf16[4,16,32,128]{3,2,1,0:T(8,128)(2,1)} %bitcast.83), calls=%async_computation.1 | async-start | bytes 1048576 | tf_op jit(solution)/shard_map/all_to_all | solution.py:174
  78.0 137.3 %all-reduce.3.cloned.1.call-start = ((), (), s32[]{:S(2)}) async-start(), calls=%async_computation.8 | async-start | bytes 8388608 | tf_op jit(solution)/shard_map/psum | solution.py:176
  85.9 22.4 %copy-start.6 = (f32[4,4,8192]{2,1,0:T(4,128)S(1)}, f32[4,4,8192]{2,1,0:T(4,128)}, u32[]{:S(2)}) copy-start(f32[4,4,8192]{2,1,0:T(4,128)} %param.18) | copy-start | bytes 1572868
  103.8 29.7 %all-to-all-start.2 = ((bf16[4,16,32,128]{3,2,1,0:T(8,128)(2,1)}), bf16[4,16,32,128]{3,2,1,0:T(8,128)(2,1)S(1)}, u32[]{:S(2)}, u32[]{:S(2)}) async-start(bf16[4,16,32,128]{3,2,1,0:T(8,128)(2,1)} %bitcast.25), calls=%async_computation.2 | async-start | bytes 1048576 | tf_op jit(solution)/shard_map/all_to_all | solution.py:174
  108.4 30.8 %copy-start.7 = (s32[4,2,16]{2,1,0:T(2,128)S(1)}, s32[4,2,16]{2,1,0:T(2,128)}, u32[]{:S(2)}) copy-start(s32[4,2,16]{2,1,0:T(2,128)} %param.15) | copy-start | bytes 1540
  108.4 107.0 %copy-start.5 = (bf16[256,128]{1,0:T(8,128)(2,1)S(1)}, bf16[256,128]{1,0:T(8,128)(2,1)}, u32[]{:S(2)}) copy-start(bf16[256,128]{1,0:T(8,128)(2,1)} %constant.31.clone.tables) | copy-start | bytes 196612
  133.5 114.5 %all-to-all-start.3 = ((bf16[4,16,32,128]{3,2,1,0:T(8,128)(2,1)}), bf16[4,16,32,128]{3,2,1,0:T(8,128)(2,1)S(1)}, u32[]{:S(2)}, u32[]{:S(2)}) async-start(bf16[4,16,32,128]{3,2,1,0:T(8,128)(2,1)} %bitcast.35), calls=%async_computation.3 | async-start | bytes 1048576 | tf_op jit(solution)/shard_map/all_to_all | solution.py:174
  215.4 1.2 copy-start.4
  216.6 10.5 %copy-start.3 = (bf16[2,512,512]{2,1,0:T(8,128)(2,1)S(1)}, bf16[2,512,512]{2,1,0:T(8,128)(2,1)}, u32[]{:S(2)}) copy-start(bf16[2,512,512]{2,1,0:T(8,128)(2,1)} %get-tuple-element.12.used) | copy-start | bytes 3145732
  227.1 10.4 %copy-start.2 = (bf16[2,512,512]{2,1,0:T(8,128)(2,1)S(1)}, bf16[2,512,512]{2,1,0:T(8,128)(2,1)}, u32[]{:S(2)}) copy-start(bf16[2,512,512]{2,1,0:T(8,128)(2,1)} %get-tuple-element.13.used) | copy-start | bytes 3145732
  237.5 10.5 %copy-start.1 = (bf16[2,512,512]{2,1,0:T(8,128)(2,1)S(1)}, bf16[2,512,512]{2,1,0:T(8,128)(2,1)}, u32[]{:S(2)}) copy-start(bf16[2,512,512]{2,1,0:T(8,128)(2,1)} %get-tuple-element.10.used) | copy-start | bytes 3145732
Sparse Core Ops, SparseCore 0:
  9.9 30.5 all-gather.10
  42.4 27.8 all-gather.12
  72.8 27.8 all-gather.14
  102.5 27.8 all-gather.16
  133.8 81.5 all-reduce.2

commit v2 on v1

v2 whole, which is shorter than its diff:
```python
import functools

import jax
import jax.numpy as jnp
import numpy as np
from jax import lax
from jax.experimental import pallas as pl
from jax.experimental.pallas import tpu as pltpu
from jax.sharding import PartitionSpec as P

RATIO = 16
ROW_ALIGN = 16
COL_ALIGN = 128


def kernel_tables(side):
    indices = np.arange(side)
    offset = (indices[:, None] - indices[None, :]).astype(np.float32)
    taps = np.arange(-6, 7).astype(np.float32)
    total = np.sum(np.exp(-taps * taps / np.float32(8.0)))
    inside = np.abs(offset) <= 6.0
    weight = np.where(inside, np.exp(-offset * offset / np.float32(8.0)), np.float32(0.0)) / total
    smooth = weight.astype(jnp.bfloat16)
    slope = (np.float32(6.0) * offset * weight / np.float32(4.0)).astype(jnp.bfloat16)
    return np.concatenate([smooth, slope], axis=0)


def dot_nt(a, b):
    return lax.dot_general(a, b, (((1,), (1,)), ((), ())), preferred_element_type=jnp.float32)


def hat(positions, cell, frac):
    return jnp.where(
        positions == cell, 1.0 - frac, jnp.where(positions == cell + 1, frac, 0.0)
    )


def look_up(table, row_cell, col_cell, row_frac, col_frac):
    side = table.shape[0] // 2
    width = row_cell.shape[1]
    rows = lax.broadcasted_iota(jnp.int32, (table.shape[1], width), 0)
    cols = lax.broadcasted_iota(jnp.int32, (side, width), 0)
    row_weight = hat(rows, row_cell, row_frac).astype(jnp.bfloat16)
    col_weight = hat(cols, col_cell, col_frac)
    values = jnp.dot(table, row_weight, preferred_element_type=jnp.float32)
    along_x = jnp.sum(values[:side] * col_weight, axis=0, keepdims=True)
    along_y = jnp.sum(values[side:] * col_weight, axis=0, keepdims=True)
    return along_x, along_y


def tile_fields(tile, tables):
    side = tile.shape[0]
    part = dot_nt(tables, tile).astype(jnp.bfloat16)
    along_x = dot_nt(part[:side], tables[side:])
    along_y = dot_nt(part[side:], tables[:side])
    return jnp.concatenate([along_x, along_y], axis=0).astype(jnp.bfloat16)


def map_window(along_x, along_y, col_extra, side):
    cols = along_x.shape[1]
    here = lax.broadcasted_iota(jnp.int32, (side, cols), 0)
    there = lax.broadcasted_iota(jnp.int32, (side, cols), 1)
    pick = (there == here + col_extra).astype(jnp.float32).astype(jnp.bfloat16)
    return jnp.concatenate(
        [dot_nt(pick, along_x), dot_nt(pick, along_y)], axis=0
    ).astype(jnp.bfloat16)


def flipped(value, bit):
    return value + (1 - 2 * (value // (1 << bit) % 2)) * (1 << bit)


def routes(count):
    levels = count.bit_length() - 1
    return list(range(1, levels)) + [0], list(range(levels - 1, 0, -1)) + [0]


def place(owner, order):
    return sum((owner // (1 << b) % 2) * (1 << i) for i, b in enumerate(order))


class Copies:
    def __init__(self, send, recv):
        self.send, self.recv, self.used, self.started = send, recv, 0, []

    def start(self, src, dst, device):
        i = self.used
        self.used += 1
        copy = pltpu.make_async_remote_copy(
            src_ref=src,
            dst_ref=dst,
            send_sem=self.send.at[i],
            recv_sem=self.recv.at[i],
            device_id=device,
            device_id_type=pl.DeviceIdType.MESH,
        )
        copy.start()
        self.started.append(copy)
        return copy


def copy_counts(n, nz, planes):
    levels = n.bit_length() - 1
    remote = (nz - 1) + planes * (2 * levels + (nz - 1) + 2 + 4 * (levels - 1))
    return remote, 3 * planes + nz


def body(
    n,
    nz,
    windows,
    spots,
    tables,
    density,
    maps,
    fine,
    long,
    fractions,
    deflection,
    source,
    every,
    out_strips,
    strips,
    used,
    full,
    landed,
    spots_all,
    spots_flat,
    send,
    recv,
    local,
):
    me, mz = lax.axis_index("rays"), lax.axis_index("planes")
    planes, tiles_here = density.shape[0], density.shape[1]
    part = tiles_here // 2
    levels = n.bit_length() - 1
    orders = routes(n)
    core = me % 2
    rows = used.shape[1]
    half = rows // 2
    blocks = windows.shape[2]
    side = tables.shape[1]
    width = fine.shape[2] // blocks
    keep = pl.multiple_of(core * half, ROW_ALIGN)
    away = pl.multiple_of((1 - core) * half, ROW_ALIGN)
    locals_used = [0]

    def local_copy(src, dst):
        copy = pltpu.make_async_copy(src, dst, local.at[locals_used[0]])
        locals_used[0] += 1
        copy.start()
        return copy

    def rays_peer(bit):
        return {"rays": flipped(me, bit), "planes": mz}

    def planes_peer(step):
        return {"rays": me, "planes": lax.rem(mz + step, nz)}

    own_spots = [place(me, order) for order in orders]
    fetched = []
    for k in range(planes):
        pair = []
        for h in range(2):
            at = (h * n + own_spots[h]) * part
            pair.append(
                local_copy(density.at[k, pl.ds(h * part, part)], every[k].at[pl.ds(at, part)])
            )
        pair.append(local_copy(maps.at[k, pl.ds(keep, half)], used.at[k, pl.ds(keep, half)]))
        fetched.append(pair)

    barrier = pltpu.get_barrier_semaphore()
    for bit in range(levels):
        pl.semaphore_signal(
            barrier, inc=1, device_id=rays_peer(bit), device_id_type=pl.DeviceIdType.MESH
        )
    for step in range(1, nz):
        pl.semaphore_signal(
            barrier, inc=1, device_id=planes_peer(step), device_id_type=pl.DeviceIdType.MESH
        )
    pl.semaphore_wait(barrier, levels + nz - 1)

    copies = Copies(send, recv)
    spot_copies = [
        copies.start(spots, spots_all.at[mz], planes_peer(step)) for step in range(1, nz)
    ]

    def spread_tiles(k):
        flight = []
        for i in range(levels):
            if i == 0:
                fetched[k][0].wait()
                fetched[k][1].wait()
            for copy in flight:
                copy.wait_recv()
            flight = []
            for h, order in enumerate(orders):
                base = own_spots[h] // (1 << i) * (1 << i)
                area = every[k].at[pl.ds((h * n + base) * part, part << i)]
                flight.append(copies.start(area, area, rays_peer(order[i])))
            yield
        for copy in flight:
            copy.wait_recv()
        if k == 0:
            for copy in spot_copies:
                copy.wait_recv()
            loads = [local_copy(spots, spots_flat.at[mz])]
            for step in range(1, nz):
                there = lax.rem(mz + step, nz)
                loads.append(local_copy(spots_all.at[there], spots_flat.at[there]))
            for load in loads:
                load.wait()
        flight = []
        for step in range(nz):
            there = lax.rem(mz + step, nz)

            def gather(b, carry):
                strip = every[k][spots_flat[there, k, b]]
                if step == 0:
                    strips[k, mz, b] = strip
                else:
                    out_strips[k, step - 1, b] = strip
                return carry

            lax.fori_loop(0, blocks, gather, 0)
            if step > 0:
                flight.append(
                    copies.start(out_strips.at[k, step - 1], strips.at[k, mz], planes_peer(step))
                )
        yield
        for copy in flight:
            copy.wait_recv()

    def spread_map(k):
        first = copies.start(maps.at[k, pl.ds(away, half)], landed.at[k, pl.ds(0, half)], rays_peer(0))
        yield
        first.wait_recv()
        fetched[k][2].wait()
        used[k, pl.ds(keep, half)] = used[k, pl.ds(keep, half)] + landed[k, pl.ds(0, half)]
        base = [core * half + h * (half // 2) for h in range(2)]
        spot = [half + h * (half // 2) for h in range(2)]
        size = half // 2
        paths = [order[:-1] for order in orders]
        for i in range(levels - 1):
            size //= 2
            flight = []
            for h in range(2):
                bit = me // (1 << paths[h][i]) % 2
                give = pl.multiple_of(base[h] + (1 - bit) * size, ROW_ALIGN)
                flight.append(
                    copies.start(
                        used.at[k, pl.ds(give, size)],
                        landed.at[k, pl.ds(spot[h], size)],
                        rays_peer(paths[h][i]),
                    )
                )
                base[h] = base[h] + bit * size
            yield
            for h in range(2):
                flight[h].wait_recv()
                at = pl.multiple_of(base[h], ROW_ALIGN)
                total = used[k, pl.ds(at, size)] + landed[k, pl.ds(spot[h], size)]
                if i < levels - 2:
                    used[k, pl.ds(at, size)] = total
                else:
                    full[k][pl.ds(at, size)] = total
                spot[h] += size
        for i in reversed(range(levels - 1)):
            flight = []
            for h in range(2):
                area = full[k].at[pl.ds(pl.multiple_of(base[h], ROW_ALIGN), size)]
                flight.append(copies.start(area, area, rays_peer(paths[h][i])))
                base[h] = base[h] - (me // (1 << paths[h][i]) % 2) * size
            yield
            size *= 2
            for copy in flight:
                copy.wait_recv()
        area = full[k].at[pl.ds(keep, half)]
        last = copies.start(area, area, rays_peer(0))
        yield
        last.wait_recv()

    chunks = map_side_chunks(rows, side)
    map_rows = rows // (2 * chunks)

    def compute(k):
        def one(b, carry):
            rays = pl.ds(pl.multiple_of(b * width, width), width)
            tile = strips[k, :, b].reshape(side, side)
            fields = tile_fields(tile, tables[...])

            span = side + ROW_ALIGN
            pieces = []
            for comp in range(2):
                pieces.append(
                    jnp.concatenate(
                        [
                            full[k][
                                pl.ds(
                                    windows[k, 0, b] * ROW_ALIGN + (comp * chunks + j) * map_rows,
                                    span,
                                )
                            ]
                            for j in range(2)
                        ],
                        axis=1,
                    )
                )
            window = map_window(pieces[0], pieces[1], windows[k, 2, b], side)
            row_extra = windows[k, 1, b]
            frac = fractions[k, :, rays]
            shift_x = jnp.zeros_like(frac[0:1])
            shift_y = shift_x
            for j in range(k):
                earlier = deflection[j, :, rays]
                shift_x = shift_x - ((k - j) / k) * earlier[0:1]
                shift_y = shift_y - ((k - j) / k) * earlier[1:2]
            fine_cell, long_cell = fine[k, :, rays], long[k, :, rays]
            fine_x, fine_y = look_up(
                fields, fine_cell[0:1], fine_cell[1:2], frac[0:1] + shift_x, frac[1:2] + shift_y
            )
            long_x, long_y = look_up(
                window,
                long_cell[0:1] + row_extra,
                long_cell[1:2],
                frac[2:3] + shift_x / RATIO,
                frac[3:4] + shift_y / RATIO,
            )
            value = jnp.concatenate([fine_x + long_x, fine_y + long_y], axis=0)
            deflection[k, :, rays] = value
            if k == planes - 1:
                total = jnp.zeros_like(value)
                for j in range(k):
                    total = total - ((planes - j) / planes) * deflection[j, :, rays]
                source[:, rays] = total - (1 / planes) * value
            return carry

        lax.fori_loop(0, blocks, one, 0)

    active = {}
    waiting = list(range(planes))
    while active or waiting:
        if waiting:
            k = waiting.pop(0)
            active[k] = [spread_tiles(k), spread_map(k)]
        ready = []
        for k in list(active):
            active[k] = [g for g in active[k] if next(g, True) is None]
            if not active[k]:
                del active[k]
                ready.append(k)
        for k in ready:
            compute(k)
    for copy in copies.started:
        copy.wait_send()


def map_side_chunks(rows, side):
    chunks = 1
    while 2 * chunks * chunks * side < rows:
        chunks += 1
    return chunks


def per_device(
    n,
    nz,
    tile_density,
    long_maps,
    map_owner,
    tile_lists,
    block_slots,
    block_windows,
    fine_cells,
    long_cells,
    fractions,
):
    my_row = lax.axis_index("rays")
    planes, tiles_here, strip_rows, side = tile_density.shape
    map_side = long_maps.shape[2]
    rays_here = fine_cells.shape[2]
    blocks = block_slots.shape[1]
    part = tiles_here // 2
    chunks = map_side // COL_ALIGN
    map_rows = 2 * chunks * map_side
    tables = jnp.asarray(kernel_tables(side))

    lists = lax.dynamic_index_in_dim(tile_lists, my_row, 0, keepdims=False)
    tiles = jnp.take_along_axis(lists, block_slots, axis=1)
    owner, inside = tiles // tiles_here, tiles % tiles_here
    order_a, order_b = routes(n)
    spot_a = place(owner, order_a) * part + inside
    spot_b = (n + place(owner, order_b)) * part + inside - part
    spots = jnp.where(inside < part, spot_a, spot_b)
    spots = jnp.pad(spots, ((0, 8 - planes), (0, 128 - blocks)))
    row_at, col_at = block_windows[:, 0], block_windows[:, 1]
    row_base = jnp.minimum(row_at // ROW_ALIGN, (map_side - side) // ROW_ALIGN - 1)
    col_base = jnp.minimum(col_at // COL_ALIGN, chunks - 2)
    windows = jnp.stack(
        [
            row_base + col_base * (map_side // ROW_ALIGN),
            row_at - row_base * ROW_ALIGN,
            col_at - col_base * COL_ALIGN,
        ],
        axis=1,
    )

    mine = (map_owner == my_row)[:, None, None, None, None]
    own = long_maps[0].reshape(planes, map_side, 2, chunks, COL_ALIGN)
    own = jnp.transpose(own, (0, 2, 3, 1, 4))
    own = jnp.where(mine, own, jnp.zeros_like(own)).reshape(planes, map_rows, COL_ALIGN)

    remote, local = copy_counts(n, nz, planes)
    vmem = pl.BlockSpec(memory_space=pltpu.VMEM)
    smem = pl.BlockSpec(memory_space=pltpu.SMEM)
    anywhere = pl.BlockSpec(memory_space=pl.ANY)
    kind = tile_density.dtype
    return pl.pallas_call(
        functools.partial(body, n, nz),
        out_shape=[
            jax.ShapeDtypeStruct((planes, 2, rays_here), jnp.float32),
            jax.ShapeDtypeStruct((2, rays_here), jnp.float32),
        ],
        in_specs=[smem, vmem, vmem, anywhere, anywhere, vmem, vmem, vmem],
        out_specs=[vmem, vmem],
        scratch_shapes=[
            [pltpu.VMEM((n * tiles_here, strip_rows, side), kind)] * planes,
            pltpu.VMEM((planes, nz - 1, blocks, strip_rows, side), kind),
            pltpu.VMEM((planes, nz, blocks, strip_rows, side), kind),
            pltpu.VMEM((planes, map_rows, COL_ALIGN), kind),
            [pltpu.VMEM((map_rows, COL_ALIGN), kind)] * planes,
            pltpu.VMEM((planes, map_rows, COL_ALIGN), kind),
            pltpu.VMEM((nz,) + spots.shape, jnp.int32),
            pltpu.SMEM((nz,) + spots.shape, jnp.int32),
            pltpu.SemaphoreType.DMA((remote,)),
            pltpu.SemaphoreType.DMA((remote,)),
            pltpu.SemaphoreType.DMA((local,)),
        ],
        compiler_params=pltpu.CompilerParams(
            collective_id=0, has_side_effects=True, vmem_limit_bytes=52 * 1024 * 1024
        ),
        cost_estimate=pl.CostEstimate(
            flops=6 * planes * rays_here * 128 * 256, bytes_accessed=16 << 20, transcendentals=0
        ),
    )(windows, spots, tables, tile_density, own, fine_cells, long_cells, fractions)


def solution(mesh):
    return jax.shard_map(
        functools.partial(per_device, mesh.shape["rays"], mesh.shape["planes"]),
        mesh=mesh,
        in_specs=(
            P(None, "rays", "planes", None),
            P("rays", None, None, None, None),
            P(),
            P(),
            P(None, ("rays", "planes")),
            P(None, None, ("rays", "planes")),
            P(None, None, ("rays", "planes")),
            P(None, None, ("rays", "planes")),
            P(None, None, ("rays", "planes")),
        ),
        out_specs=(P(None, None, ("rays", "planes")), P(None, ("rays", "planes"))),
        check_vma=False,
    )
```

time: 267 us -> 131 us (0.49)
  waiting for transfers between devices: 144 us -> 0 us
  Pallas kernels: 42.4 us -> 112 us
  starting transfers between devices: 18.6 us -> 0 us
  local copies, waits for them, and re-layouts: 25.9 us -> 10 us
  blocking collectives: 13.5 us -> 0 us
  between operations: 14 us -> 0.69 us
    psum x1 -> x0, waiting for transfers between devices: 76.2 us -> none  [per_device(): used = lax.psum(jnp.where(mine[plane], own, jnp.zeros_like(own)), 'rays')]
    pallas_call x4 -> x1, Pallas kernels: 42.4 us -> 112 us  [per_device(): pl.pallas_call(functools.partial(body, n, nz), out_shape=[jax.ShapeDtypeS...]
    all_gather x4 -> x0, waiting for transfers between devices: 65.8 us -> none  [per_device(): every = lax.all_gather(tile_density[plane], 'rays', axis=0, tiled=True)]
    all_to_all x4 -> x0, starting transfers between devices: 18.4 us -> none  [per_device(): lax.all_to_all(out, 'planes', split_axis=0, concat_axis=0, tiled=True)]
    gather x7 -> x3, local copies, waits for them, and re-layouts: 14.8 us -> 1.05 us  [per_device(): tiles = jnp.take_along_axis(lists, block_slots, axis=1)]
    all_gather x1 -> x0, blocking collectives: 13.5 us -> none  [per_device(): slots = lax.all_gather(block_slots, 'planes', axis=0)]
    another operation x0 -> x1, local copies, waits for them, and re-layouts: none -> 7.57 us  [per_device(): own = long_maps[0].reshape(planes, map_side, 2, chunks, COL_ALIGN)]
    slice x3 -> x0, local copies, waits for them, and re-layouts: 6.18 us -> none  [the longest x1 5.55 us: per_device(): own = jnp.transpose(long_maps[0, plane], (1, 0, 2))]
  transfers between devices with their start and end apart: 9 -> 0, of which waited for: 5 -> 0; matrix products, arithmetic and copies ran while one was open for 11% -> 0% of each run, Pallas kernels for 12% -> 0%
where the time goes in v2:
time: 131 us
  Pallas kernels  112 us (85%)
  local copies, waits for them, and re-layouts  10 us (8%)
  other arithmetic  8.59 us (7%)
    pallas_call x1, Pallas kernels, per_device(): pl.pallas_call(functools.partial(body, n, nz), out_shape=[jax.ShapeDtypeS...  112 us
    another operation x1, local copies, waits for them, and re-layouts, per_device(): own = long_maps[0].reshape(planes, map_side, 2, chunks, COL_ALIGN)  7.57 us
    select_n x1, other arithmetic, per_device(): jnp.where(mine, own, jnp.zeros_like(own))  4.94 us

profile of v2, /device:TPU:0, one launch (start us, length us, event | category | flops | bytes accessed | tf_op | source)
XLA Modules:
  0.0 130.8 jit_solution(12100108109590891731)
XLA Ops:
  0.6 0.0 copy-start
  0.6 0.7 broadcast_compare_fusion
  1.3 0.0 copy-done
  1.4 0.7 bitcast_or_fusion
  2.0 0.1 reshape.19
  2.1 0.9 gather_fusion
  3.0 0.1 reshape.22
  3.1 0.7 add_select_fusion.7
  3.8 0.8 multiply_add_fusion
  4.6 0.8 multiply_subtract_fusion.1
  5.4 7.6 %reshape_squeeze.3 = bf16[4,512,2,4,128]{4,3,2,1,0:T(4,128)(2,1)} reshape(bf16[1,4,512,2,512]{4,3,2,1,0:T(2,128)(2,1)} %param.11) | data formatting | bytes 8388608 | tf_op jit(solution)/shard_map/reshape;squeeze | solution.py:409
  13.0 0.0 copy-start.1
  13.0 0.0 copy-start.2
  13.0 0.0 copy-start.3
  13.0 0.0 copy-start.4
  13.0 4.9 %copy_select_fusion = bf16[4,512,2,4,128]{4,1,3,2,0:T(8,128)(2,1)} fusion(bf16[4,512,2,4,128]{4,3,2,1,0:T(4,128)(2,1)} %reshape_squeeze.3, pred[4]{0:T(512)(128)(4,1)S(1)} %broadcast_compare_fusion), kind=kLoop, calls=%fused_computation.1 | loop fusion | flops 2097152 | bytes 8388612 | tf_op jit(solution)/shard_map/jit(_where)/select_n | solution.py:411
  17.9 0.0 copy-done.1
  17.9 0.0 copy-done.2
  17.9 0.0 copy-done.3
  17.9 0.0 copy-done.4
  18.0 111.5 %shard_map.113 = (f32[4,2,8192]{2,1,0:T(2,128)S(1)}, f32[2,8192]{1,0:T(2,128)S(1)}) custom-call(s32[4,3,16]{2,1,0:T(4,128)S(1)} %pad_add_fusion.windows, s32[8,128]{1,0:T(8,128)S(1)} %pad.4.spots, bf16[256,128]{1,0:T(8,128)(2,1)S(1)} %copy-done.4, bf16[4,32,32,128]{3,2,1,0:T(8,128)(2,1)} %density.1, bf16[4,4096,128]{2,1,0:T(8,128)(2,1)} %bitcast.9, ...), custom_call_target="tpu_custom_call" | custom-call | flops 6442450944 | bytes 16777216 | tf_op jit(solution)/shard_map/pallas_call | solution.py:418
  129.5 0.7 copy.17
  130.2 0.6 copy.18
  (3 shorter events, 0.0 us)
Async XLA Ops:
  0.6 0.7 copy-start
  13.0 5.0 %copy-start.1 = (f32[4,4,8192]{2,1,0:T(4,128)S(1)}, f32[4,4,8192]{2,1,0:T(4,128)}, u32[]{:S(2)}) copy-start(f32[4,4,8192]{2,1,0:T(4,128)} %fractions.1) | copy-start | bytes 1572868
  13.0 5.0 %copy-start.2 = (s32[4,2,8192]{2,1,0:T(2,128)S(1)}, s32[4,2,8192]{2,1,0:T(2,128)}, u32[]{:S(2)}) copy-start(s32[4,2,8192]{2,1,0:T(2,128)} %fine.1) | copy-start | bytes 786436
  13.0 5.0 %copy-start.3 = (s32[4,2,8192]{2,1,0:T(2,128)S(1)}, s32[4,2,8192]{2,1,0:T(2,128)}, u32[]{:S(2)}) copy-start(s32[4,2,8192]{2,1,0:T(2,128)} %long.1) | copy-start | bytes 786436
  13.0 5.0 %copy-start.4 = (bf16[256,128]{1,0:T(8,128)(2,1)S(1)}, bf16[256,128]{1,0:T(8,128)(2,1)}, u32[]{:S(2)}) copy-start(bf16[256,128]{1,0:T(8,128)(2,1)} %constant.155.clone.tables) | copy-start | bytes 196612

commit v3 on v2

--- a/solution.py
+++ b/solution.py
@@ -11,6 +11,9 @@
 RATIO = 16
 ROW_ALIGN = 16
 COL_ALIGN = 128
+TILE_GROUP = 4
+MAP_GROUP = 4
+RAY_GROUP = 2
 
 
 def kernel_tables(side):
@@ -109,8 +112,10 @@
     n,
     nz,
     windows,
+    held,
     spots,
     tables,
+    unmix,
     density,
     maps,
     fine,
@@ -124,6 +129,8 @@
     used,
     full,
     landed,
+    planar,
+    fields,
     spots_all,
     spots_flat,
     send,
@@ -231,12 +238,18 @@
         for copy in flight:
             copy.wait_recv()
 
+    def choose(mine, here, there):
+        weight = jnp.full((1, here.shape[1]), mine, jnp.float32)
+        return here * weight.astype(here.dtype) + there * (1.0 - weight).astype(here.dtype)
+
     def spread_map(k):
         first = copies.start(maps.at[k, pl.ds(away, half)], landed.at[k, pl.ds(0, half)], rays_peer(0))
         yield
         first.wait_recv()
         fetched[k][2].wait()
-        used[k, pl.ds(keep, half)] = used[k, pl.ds(keep, half)] + landed[k, pl.ds(0, half)]
+        used[k, pl.ds(keep, half)] = choose(
+            held[k, 0, 0], used[k, pl.ds(keep, half)], landed[k, pl.ds(0, half)]
+        )
         base = [core * half + h * (half // 2) for h in range(2)]
         spot = [half + h * (half // 2) for h in range(2)]
         size = half // 2
@@ -259,7 +272,9 @@
             for h in range(2):
                 flight[h].wait_recv()
                 at = pl.multiple_of(base[h], ROW_ALIGN)
-                total = used[k, pl.ds(at, size)] + landed[k, pl.ds(spot[h], size)]
+                total = choose(
+                    held[k, h, i + 1], used[k, pl.ds(at, size)], landed[k, pl.ds(spot[h], size)]
+                )
                 if i < levels - 2:
                     used[k, pl.ds(at, size)] = total
                 else:
@@ -283,74 +298,105 @@
     chunks = map_side_chunks(rows, side)
     map_rows = rows // (2 * chunks)
 
+    def convolve_tiles(k):
+        def some(g, carry):
+            made = []
+            for u in range(TILE_GROUP):
+                tile = strips[k, :, g * TILE_GROUP + u].reshape(side, side)
+                made.append(tile_fields(tile, tables[...]))
+            for u in range(TILE_GROUP):
+                fields[k, g * TILE_GROUP + u] = made[u]
+            return carry
+
+        lax.fori_loop(0, blocks // TILE_GROUP, some, 0)
+
+    def separate(k):
+        kinds = 2 * chunks
+        span = side // kinds
+
+        def some(g, carry):
+            parts = []
+            for u in range(MAP_GROUP):
+                at = pl.multiple_of((g * MAP_GROUP + u) * side, side)
+                parts.append(
+                    jnp.dot(
+                        unmix[...], full[k][pl.ds(at, side)], preferred_element_type=jnp.float32
+                    ).astype(jnp.bfloat16)
+                )
+            moved = jnp.concatenate(
+                [part.reshape(kinds, span, side) for part in parts], axis=1
+            )
+            at = pl.multiple_of(g * (MAP_GROUP * span), MAP_GROUP * span)
+            for j in range(kinds):
+                planar[k, pl.ds(j * map_rows + at, MAP_GROUP * span)] = moved[j]
+            return carry
+
+        lax.fori_loop(0, rows // (side * MAP_GROUP), some, 0)
+
+    def look(k, b):
+        rays = pl.ds(pl.multiple_of(b * width, width), width)
+        span = side + ROW_ALIGN
+        pieces = []
+        for comp in range(2):
+            lanes = []
+            for j in range(2):
+                at = windows[k, 0, b] * ROW_ALIGN + (2 * j + comp) * map_rows
+                lanes.append(planar[k, pl.ds(at, span)])
+            pieces.append(jnp.concatenate(lanes, axis=1))
+        window = map_window(pieces[0], pieces[1], windows[k, 2, b], side)
+        row_extra = windows[k, 1, b]
+        frac = fractions[k, :, rays]
+        shift = jnp.zeros_like(frac[0:2])
+        for j in range(k):
+            shift = shift - ((k - j) / k) * deflection[j, :, rays]
+        shift_x, shift_y = shift[0:1], shift[1:2]
+        fine_cell, long_cell = fine[k, :, rays], long[k, :, rays]
+        fine_x, fine_y = look_up(
+            fields[k, b], fine_cell[0:1], fine_cell[1:2], frac[0:1] + shift_x, frac[1:2] + shift_y
+        )
+        long_x, long_y = look_up(
+            window,
+            long_cell[0:1] + row_extra,
+            long_cell[1:2],
+            frac[2:3] + shift_x / RATIO,
+            frac[3:4] + shift_y / RATIO,
+        )
+        value = jnp.concatenate([fine_x + long_x, fine_y + long_y], axis=0)
+        total = jnp.zeros_like(value)
+        if k == planes - 1:
+            for j in range(k):
+                total = total - ((planes - j) / planes) * deflection[j, :, rays]
+            total = total - (1 / planes) * value
+        return rays, value, total
+
     def compute(k):
-        def one(b, carry):
-            rays = pl.ds(pl.multiple_of(b * width, width), width)
-            tile = strips[k, :, b].reshape(side, side)
-            fields = tile_fields(tile, tables[...])
-
-            span = side + ROW_ALIGN
-            pieces = []
-            for comp in range(2):
-                pieces.append(
-                    jnp.concatenate(
-                        [
-                            full[k][
-                                pl.ds(
-                                    windows[k, 0, b] * ROW_ALIGN + (comp * chunks + j) * map_rows,
-                                    span,
-                                )
-                            ]
-                            for j in range(2)
-                        ],
-                        axis=1,
-                    )
-                )
-            window = map_window(pieces[0], pieces[1], windows[k, 2, b], side)
-            row_extra = windows[k, 1, b]
-            frac = fractions[k, :, rays]
-            shift_x = jnp.zeros_like(frac[0:1])
-            shift_y = shift_x
-            for j in range(k):
-                earlier = deflection[j, :, rays]
-                shift_x = shift_x - ((k - j) / k) * earlier[0:1]
-                shift_y = shift_y - ((k - j) / k) * earlier[1:2]
-            fine_cell, long_cell = fine[k, :, rays], long[k, :, rays]
-            fine_x, fine_y = look_up(
-                fields, fine_cell[0:1], fine_cell[1:2], frac[0:1] + shift_x, frac[1:2] + shift_y
-            )
-            long_x, long_y = look_up(
-                window,
-                long_cell[0:1] + row_extra,
-                long_cell[1:2],
-                frac[2:3] + shift_x / RATIO,
-                frac[3:4] + shift_y / RATIO,
-            )
-            value = jnp.concatenate([fine_x + long_x, fine_y + long_y], axis=0)
-            deflection[k, :, rays] = value
-            if k == planes - 1:
-                total = jnp.zeros_like(value)
-                for j in range(k):
-                    total = total - ((planes - j) / planes) * deflection[j, :, rays]
-                source[:, rays] = total - (1 / planes) * value
+        def some(g, carry):
+            done = [look(k, g * RAY_GROUP + u) for u in range(RAY_GROUP)]
+            for rays, value, total in done:
+                deflection[k, :, rays] = value
+                if k == planes - 1:
+                    source[:, rays] = total
             return carry
 
-        lax.fori_loop(0, blocks, one, 0)
+        lax.fori_loop(0, blocks // RAY_GROUP, some, 0)
 
     active = {}
     waiting = list(range(planes))
     while active or waiting:
         if waiting:
             k = waiting.pop(0)
-            active[k] = [spread_tiles(k), spread_map(k)]
+            active[k] = {convolve_tiles: spread_tiles(k), separate: spread_map(k)}
         ready = []
         for k in list(active):
-            active[k] = [g for g in active[k] if next(g, True) is None]
+            for after, steps in list(active[k].items()):
+                if next(steps, True) is True:
+                    del active[k][after]
+                    ready.append((after, k))
             if not active[k]:
                 del active[k]
-                ready.append(k)
-        for k in ready:
-            compute(k)
+                ready.append((compute, k))
+        for after, k in ready:
+            after(k)
     for copy in copies.started:
         copy.wait_send()
 
@@ -386,7 +432,8 @@
     tables = jnp.asarray(kernel_tables(side))
 
     lists = lax.dynamic_index_in_dim(tile_lists, my_row, 0, keepdims=False)
-    tiles = jnp.take_along_axis(lists, block_slots, axis=1)
+    picked = block_slots[:, :, None] == jnp.arange(lists.shape[1], dtype=jnp.int32)
+    tiles = jnp.sum(jnp.where(picked, lists[:, None, :], 0), axis=2)
     owner, inside = tiles // tiles_here, tiles % tiles_here
     order_a, order_b = routes(n)
     spot_a = place(owner, order_a) * part + inside
@@ -398,17 +445,27 @@
     col_base = jnp.minimum(col_at // COL_ALIGN, chunks - 2)
     windows = jnp.stack(
         [
-            row_base + col_base * (map_side // ROW_ALIGN),
+            row_base + 2 * col_base * (map_side // ROW_ALIGN),
             row_at - row_base * ROW_ALIGN,
             col_at - col_base * COL_ALIGN,
         ],
         axis=1,
     )
 
-    mine = (map_owner == my_row)[:, None, None, None, None]
     own = long_maps[0].reshape(planes, map_side, 2, chunks, COL_ALIGN)
-    own = jnp.transpose(own, (0, 2, 3, 1, 4))
-    own = jnp.where(mine, own, jnp.zeros_like(own)).reshape(planes, map_rows, COL_ALIGN)
+    own = jnp.transpose(own, (0, 1, 3, 2, 4)).reshape(planes, map_rows, COL_ALIGN)
+    unlike = map_owner[:, None, None] ^ my_row
+    levels = n.bit_length() - 1
+    reached = [
+        [sum(1 << b for b in ([0] + order[:-1])[:i]) for i in range(levels)]
+        for order in (order_a, order_b)
+    ]
+    apart = jnp.asarray([[n - 1 - r for r in row] for row in reached], jnp.int32)
+    held = ((unlike & apart) == 0).astype(jnp.float32)
+    kinds = 2 * chunks
+    span = side // kinds
+    to = np.arange(side)
+    unmix = (to[None, :] == (to[:, None] % span) * kinds + to[:, None] // span).astype(jnp.bfloat16)
 
     remote, local = copy_counts(n, nz, planes)
     vmem = pl.BlockSpec(memory_space=pltpu.VMEM)
@@ -421,7 +478,7 @@
             jax.ShapeDtypeStruct((planes, 2, rays_here), jnp.float32),
             jax.ShapeDtypeStruct((2, rays_here), jnp.float32),
         ],
-        in_specs=[smem, vmem, vmem, anywhere, anywhere, vmem, vmem, vmem],
+        in_specs=[smem, smem, vmem, vmem, vmem, anywhere, anywhere, vmem, vmem, vmem],
         out_specs=[vmem, vmem],
         scratch_shapes=[
             [pltpu.VMEM((n * tiles_here, strip_rows, side), kind)] * planes,
@@ -430,6 +487,8 @@
             pltpu.VMEM((planes, map_rows, COL_ALIGN), kind),
             [pltpu.VMEM((map_rows, COL_ALIGN), kind)] * planes,
             pltpu.VMEM((planes, map_rows, COL_ALIGN), kind),
+            pltpu.VMEM((planes, map_rows, COL_ALIGN), kind),
+            pltpu.VMEM((planes, blocks, 2 * side, side), kind),
             pltpu.VMEM((nz,) + spots.shape, jnp.int32),
             pltpu.SMEM((nz,) + spots.shape, jnp.int32),
             pltpu.SemaphoreType.DMA((remote,)),
@@ -442,7 +501,7 @@
         cost_estimate=pl.CostEstimate(
             flops=6 * planes * rays_here * 128 * 256, bytes_accessed=16 << 20, transcendentals=0
         ),
-    )(windows, spots, tables, tile_density, own, fine_cells, long_cells, fractions)
+    )(windows, held, spots, tables, jnp.asarray(unmix), tile_density, own, fine_cells, long_cells, fractions)
 
 
 def solution(mesh):

time: 131 us -> 121 us (0.924)
  other arithmetic: 8.59 us -> 3.92 us
  local copies, waits for them, and re-layouts: 10 us -> 5.93 us
  Pallas kernels: 112 us -> 110 us
    another operation x1 -> x0, local copies, waits for them, and re-layouts: 7.57 us -> none  [per_device(): own = long_maps[0].reshape(planes, map_side, 2, chunks, COL_ALIGN)]
    select_n x1 -> x0, other arithmetic: 4.94 us -> none  [per_device(): jnp.where(mine, own, jnp.zeros_like(own))]
    unnamed x12 -> x14, local copies, waits for them, and re-layouts: 1.4 us -> 5.92 us
    pallas_call x1, Pallas kernels: 112 us -> 110 us  [per_device(): pl.pallas_call(functools.partial(body, n, nz), out_shape=[jax.ShapeDtypeS...]
where the time goes in v3:
time: 121 us; the launch traced here: 120 us
  Pallas kernels  110 us (91%)
  local copies, waits for them, and re-layouts  5.93 us (5%)
  other arithmetic  3.92 us (3%)
    pallas_call x1, Pallas kernels, per_device(): pl.pallas_call(functools.partial(body, n, nz), out_shape=[jax.ShapeDtypeS...  110 us
    unnamed x14, local copies, waits for them, and re-layouts  5.92 us

profile of v3, /device:TPU:0, one launch (start us, length us, event | category | flops | bytes accessed | tf_op | source)
XLA Modules:
  0.0 120.2 jit_solution(12352035837606264219)
XLA Ops:
  0.6 0.0 copy-start
  0.6 0.7 broadcast_xor_fusion
  1.3 0.0 copy-done
  1.4 0.9 select_reduce_fusion
  2.3 0.8 compare_convert_fusion.held
  3.1 0.8 multiply_add_fusion
  3.9 0.8 multiply_subtract_fusion.1
  4.6 0.0 copy-start.1
  4.7 1.0 copy-done.1
  5.7 0.0 copy-start.2
  5.7 0.9 copy-done.2
  6.6 0.0 copy-start.3
  6.6 0.9 copy-done.3
  7.6 0.0 copy-start.4
  7.6 0.8 copy-done.4
  8.4 0.0 copy-start.5
  8.4 0.8 copy-done.5
  9.2 109.6 %shard_map.131 = (f32[4,2,8192]{2,1,0:T(2,128)S(1)}, f32[2,8192]{1,0:T(2,128)S(1)}) custom-call(s32[4,3,16]{2,1,0:T(4,128)S(1)} %pad_add_fusion.windows, f32[4,2,3]{2,1,0:T(2,128)S(1)} %compare_convert_fusion.held, s32[8,128]{1,0:T(8,128)S(1)} %pad.4.spots, bf16[256,128]{1,0:T(8,128)(2,1)S(1)} %copy-done.4, bf16[128,128]{1,0:T(8,128)(2,1)S(1)} %copy-done.5, ...), custom_call_target="tpu_custom_call" | custom-call | flops 6442450944 | bytes 16777216 | tf_op jit(solution)/shard_map/pallas_call | solution.py:475
  118.8 0.7 copy.18
  119.5 0.6 copy.19
  (4 shorter events, 0.1 us)
Async XLA Ops:
  0.6 0.7 copy-start
  4.6 1.0 copy-start.1
  5.7 0.9 copy-start.2
  6.6 0.9 copy-start.3
  7.6 0.8 copy-start.4
  8.4 0.8 copy-start.5

commit v4 on v3

--- a/solution.py
+++ b/solution.py
@@ -14,6 +14,8 @@
 TILE_GROUP = 4
 MAP_GROUP = 4
 RAY_GROUP = 2
+SHARES = 4
+MAP_LEAD = 1
 
 
 def kernel_tables(side):
@@ -38,12 +40,22 @@
     )
 
 
+def hat_rounded(positions, cell, frac):
+    here = cell.astype(jnp.float32).astype(jnp.bfloat16)
+    there = (cell + 1).astype(jnp.float32).astype(jnp.bfloat16)
+    low = (1.0 - frac).astype(jnp.bfloat16)
+    high = frac.astype(jnp.bfloat16)
+    none = jnp.zeros_like(high)
+    return jnp.where(positions == here, low, jnp.where(positions == there, high, none))
+
+
 def look_up(table, row_cell, col_cell, row_frac, col_frac):
     side = table.shape[0] // 2
     width = row_cell.shape[1]
     rows = lax.broadcasted_iota(jnp.int32, (table.shape[1], width), 0)
+    rows = rows.astype(jnp.float32).astype(jnp.bfloat16)
     cols = lax.broadcasted_iota(jnp.int32, (side, width), 0)
-    row_weight = hat(rows, row_cell, row_frac).astype(jnp.bfloat16)
+    row_weight = hat_rounded(rows, row_cell, row_frac)
     col_weight = hat(cols, col_cell, col_frac)
     values = jnp.dot(table, row_weight, preferred_element_type=jnp.float32)
     along_x = jnp.sum(values[:side] * col_weight, axis=0, keepdims=True)
@@ -105,7 +117,7 @@
 def copy_counts(n, nz, planes):
     levels = n.bit_length() - 1
     remote = (nz - 1) + planes * (2 * levels + (nz - 1) + 2 + 4 * (levels - 1))
-    return remote, 3 * planes + nz
+    return remote, 3 * planes + nz + 3
 
 
 def body(
@@ -118,11 +130,14 @@
     unmix,
     density,
     maps,
+    fine_in,
+    long_in,
+    fractions_in,
+    deflection,
+    source,
     fine,
     long,
     fractions,
-    deflection,
-    source,
     every,
     out_strips,
     strips,
@@ -147,7 +162,7 @@
     half = rows // 2
     blocks = windows.shape[2]
     side = tables.shape[1]
-    width = fine.shape[2] // blocks
+    width = fine_in.shape[2] // blocks
     keep = pl.multiple_of(core * half, ROW_ALIGN)
     away = pl.multiple_of((1 - core) * half, ROW_ALIGN)
     locals_used = [0]
@@ -175,6 +190,12 @@
             )
         pair.append(local_copy(maps.at[k, pl.ds(keep, half)], used.at[k, pl.ds(keep, half)]))
         fetched.append(pair)
+
+    ray_loads = [
+        local_copy(fine_in, fine),
+        local_copy(long_in, long),
+        local_copy(fractions_in, fractions),
+    ]
 
     barrier = pltpu.get_barrier_semaphore()
     for bit in range(levels):
@@ -369,7 +390,12 @@
             total = total - (1 / planes) * value
         return rays, value, total
 
-    def compute(k):
+    def compute(k, share):
+        if k == 0 and share == 0:
+            for load in ray_loads:
+                load.wait()
+        groups = blocks // RAY_GROUP // SHARES
+
         def some(g, carry):
             done = [look(k, g * RAY_GROUP + u) for u in range(RAY_GROUP)]
             for rays, value, total in done:
@@ -378,25 +404,27 @@
                     source[:, rays] = total
             return carry
 
-        lax.fori_loop(0, blocks // RAY_GROUP, some, 0)
-
-    active = {}
-    waiting = list(range(planes))
-    while active or waiting:
-        if waiting:
-            k = waiting.pop(0)
-            active[k] = {convolve_tiles: spread_tiles(k), separate: spread_map(k)}
-        ready = []
-        for k in list(active):
-            for after, steps in list(active[k].items()):
-                if next(steps, True) is True:
-                    del active[k][after]
-                    ready.append((after, k))
-            if not active[k]:
-                del active[k]
-                ready.append((compute, k))
-        for after, k in ready:
-            after(k)
+        lax.fori_loop(share * groups, (share + 1) * groups, some, 0)
+
+    chains = {}
+    for k in range(planes):
+        chains[k, 0] = (max(0, k - MAP_LEAD), spread_map(k), separate)
+        chains[k, 1] = (k, spread_tiles(k), convolve_tiles)
+    jobs, left, moment = [], [2] * planes, 0
+    while chains:
+        for key in list(chains):
+            begin, steps, after = chains[key]
+            if moment >= begin and next(steps, True) is True:
+                del chains[key]
+                jobs.append(functools.partial(after, key[0]))
+                left[key[0]] -= 1
+                if left[key[0]] == 0:
+                    jobs += [functools.partial(compute, key[0], i) for i in range(SHARES)]
+            if jobs:
+                jobs.pop(0)()
+        moment += 1
+    for job in jobs:
+        job()
     for copy in copies.started:
         copy.wait_send()
 
@@ -478,9 +506,12 @@
             jax.ShapeDtypeStruct((planes, 2, rays_here), jnp.float32),
             jax.ShapeDtypeStruct((2, rays_here), jnp.float32),
         ],
-        in_specs=[smem, smem, vmem, vmem, vmem, anywhere, anywhere, vmem, vmem, vmem],
+        in_specs=[smem, smem, vmem, vmem, vmem, anywhere, anywhere, anywhere, anywhere, anywhere],
         out_specs=[vmem, vmem],
         scratch_shapes=[
+            pltpu.VMEM(fine_cells.shape, fine_cells.dtype),
+            pltpu.VMEM(long_cells.shape, long_cells.dtype),
+            pltpu.VMEM(fractions.shape, fractions.dtype),
             [pltpu.VMEM((n * tiles_here, strip_rows, side), kind)] * planes,
             pltpu.VMEM((planes, nz - 1, blocks, strip_rows, side), kind),
             pltpu.VMEM((planes, nz, blocks, strip_rows, side), kind),

time: 121 us -> 124 us (1.025); the launches traced: 120 us -> 121 us
  no operation moved by 1% of the time
where the time goes in v4:
time: 124 us; the launch traced here: 121 us
  Pallas kernels  111 us (90%)
  local copies, waits for them, and re-layouts  5.93 us (5%)
  other arithmetic  3.92 us (3%)
    pallas_call x1, Pallas kernels, per_device(): pl.pallas_call(functools.partial(body, n, nz), out_shape=[jax.ShapeDtypeS...  111 us
    unnamed x14, local copies, waits for them, and re-layouts  5.92 us

profile of v4, /device:TPU:0, one launch (start us, length us, event | category | flops | bytes accessed | tf_op | source)
XLA Modules:
  0.0 121.3 jit_solution(8243365393981561211)
XLA Ops:
  0.6 0.0 copy-start
  0.6 0.7 broadcast_xor_fusion
  1.3 0.0 copy-done
  1.4 0.9 select_reduce_fusion
  2.3 0.8 compare_convert_fusion.held
  3.1 0.8 multiply_add_fusion
  3.9 0.8 multiply_subtract_fusion.1
  4.6 0.0 copy-start.1
  4.7 1.0 copy-done.1
  5.7 0.0 copy-start.2
  5.7 0.9 copy-done.2
  6.6 0.0 copy-start.3
  6.6 0.9 copy-done.3
  7.6 0.0 copy-start.4
  7.6 0.8 copy-done.4
  8.4 0.0 copy-start.5
  8.4 0.8 copy-done.5
  9.2 110.8 %shard_map.131 = (f32[4,2,8192]{2,1,0:T(2,128)S(1)}, f32[2,8192]{1,0:T(2,128)S(1)}) custom-call(s32[4,3,16]{2,1,0:T(4,128)S(1)} %pad_add_fusion.windows, f32[4,2,3]{2,1,0:T(2,128)S(1)} %compare_convert_fusion.held, s32[8,128]{1,0:T(8,128)S(1)} %pad.4.spots, bf16[256,128]{1,0:T(8,128)(2,1)S(1)} %copy-done.4, bf16[128,128]{1,0:T(8,128)(2,1)S(1)} %copy-done.5, ...), custom_call_target="tpu_custom_call" | custom-call | flops 6442450944 | bytes 16777216 | tf_op jit(solution)/shard_map/pallas_call | solution.py:503
  120.0 0.7 copy.18
  120.7 0.6 copy.19
  (4 shorter events, 0.1 us)
Async XLA Ops:
  0.6 0.7 copy-start
  4.6 1.0 copy-start.1
  5.7 0.9 copy-start.2
  6.6 0.9 copy-start.3
  7.6 0.8 copy-start.4
  8.4 0.8 copy-start.5

commit v5 on v4

--- a/solution.py
+++ b/solution.py
@@ -15,7 +15,8 @@
 MAP_GROUP = 4
 RAY_GROUP = 2
 SHARES = 4
-MAP_LEAD = 1
+PAIR = 2
+PAIR_GAP = 2
 
 
 def kernel_tables(side):
@@ -124,7 +125,7 @@
     n,
     nz,
     windows,
-    held,
+    owners,
     spots,
     tables,
     unmix,
@@ -259,8 +260,10 @@
         for copy in flight:
             copy.wait_recv()
 
-    def choose(mine, here, there):
-        weight = jnp.full((1, here.shape[1]), mine, jnp.float32)
+    def choose(k, done, here, there):
+        apart = n - 1 - sum(1 << bit for bit in done)
+        unlike = jnp.bitwise_and(jnp.bitwise_xor(owners[k], me), apart)
+        weight = jnp.where(jnp.full((1, here.shape[1]), unlike) == 0, 1.0, 0.0)
         return here * weight.astype(here.dtype) + there * (1.0 - weight).astype(here.dtype)
 
     def spread_map(k):
@@ -269,7 +272,7 @@
         first.wait_recv()
         fetched[k][2].wait()
         used[k, pl.ds(keep, half)] = choose(
-            held[k, 0, 0], used[k, pl.ds(keep, half)], landed[k, pl.ds(0, half)]
+            k, [], used[k, pl.ds(keep, half)], landed[k, pl.ds(0, half)]
         )
         base = [core * half + h * (half // 2) for h in range(2)]
         spot = [half + h * (half // 2) for h in range(2)]
@@ -294,7 +297,7 @@
                 flight[h].wait_recv()
                 at = pl.multiple_of(base[h], ROW_ALIGN)
                 total = choose(
-                    held[k, h, i + 1], used[k, pl.ds(at, size)], landed[k, pl.ds(spot[h], size)]
+                    k, [0] + paths[h][:i], used[k, pl.ds(at, size)], landed[k, pl.ds(spot[h], size)]
                 )
                 if i < levels - 2:
                     used[k, pl.ds(at, size)] = total
@@ -408,8 +411,9 @@
 
     chains = {}
     for k in range(planes):
-        chains[k, 0] = (max(0, k - MAP_LEAD), spread_map(k), separate)
-        chains[k, 1] = (k, spread_tiles(k), convolve_tiles)
+        begin = k // PAIR * PAIR_GAP
+        chains[k, 0] = (begin, spread_tiles(k), convolve_tiles)
+        chains[k, 1] = (begin, spread_map(k), separate)
     jobs, left, moment = [], [2] * planes, 0
     while chains:
         for key in list(chains):
@@ -482,14 +486,6 @@
 
     own = long_maps[0].reshape(planes, map_side, 2, chunks, COL_ALIGN)
     own = jnp.transpose(own, (0, 1, 3, 2, 4)).reshape(planes, map_rows, COL_ALIGN)
-    unlike = map_owner[:, None, None] ^ my_row
-    levels = n.bit_length() - 1
-    reached = [
-        [sum(1 << b for b in ([0] + order[:-1])[:i]) for i in range(levels)]
-        for order in (order_a, order_b)
-    ]
-    apart = jnp.asarray([[n - 1 - r for r in row] for row in reached], jnp.int32)
-    held = ((unlike & apart) == 0).astype(jnp.float32)
     kinds = 2 * chunks
     span = side // kinds
     to = np.arange(side)
@@ -527,12 +523,12 @@
             pltpu.SemaphoreType.DMA((local,)),
         ],
         compiler_params=pltpu.CompilerParams(
-            collective_id=0, has_side_effects=True, vmem_limit_bytes=52 * 1024 * 1024
+            collective_id=0, has_side_effects=True, vmem_limit_bytes=62 * 1024 * 1024
         ),
         cost_estimate=pl.CostEstimate(
             flops=6 * planes * rays_here * 128 * 256, bytes_accessed=16 << 20, transcendentals=0
         ),
-    )(windows, held, spots, tables, jnp.asarray(unmix), tile_density, own, fine_cells, long_cells, fractions)
+    )(windows, map_owner, spots, tables, jnp.asarray(unmix), tile_density, own, fine_cells, long_cells, fractions)
 
 
 def solution(mesh):

time: 124 us -> 125 us (level); the launches traced: 121 us -> 125 us
  Pallas kernels: 111 us -> 117 us
  local copies, waits for them, and re-layouts: 5.93 us -> 4.45 us
    pallas_call x1, Pallas kernels: 111 us -> 117 us  [per_device(): pl.pallas_call(functools.partial(body, n, nz), out_shape=[jax.ShapeDtypeS...]
    unnamed x14 -> x4, local copies, waits for them, and re-layouts: 5.92 us -> 3.85 us
where the time goes in v5:
time: 125 us
  Pallas kernels  117 us (94%)
  local copies, waits for them, and re-layouts  4.45 us (4%)
  other arithmetic  3.1 us (2%)
    pallas_call x1, Pallas kernels, per_device(): pl.pallas_call(functools.partial(body, n, nz), out_shape=[jax.ShapeDtypeS...  117 us
    unnamed x4, local copies, waits for them, and re-layouts  3.85 us

profile of v5, /device:TPU:0, one launch (start us, length us, event | category | flops | bytes accessed | tf_op | source)
XLA Modules:
  0.0 125.1 jit_solution(6490504424978247577)
XLA Ops:
  0.6 0.0 copy-start
  0.6 0.7 copy-done
  1.4 0.9 select_reduce_fusion
  2.3 0.6 pad.4.spots
  2.9 0.8 multiply_add_fusion
  3.7 0.8 multiply_subtract_fusion.1
  4.5 0.6 pad_add_fusion.windows
  5.1 116.8 %shard_map.122 = (f32[4,2,8192]{2,1,0:T(2,128)}, f32[2,8192]{1,0:T(2,128)}) custom-call(s32[4,3,16]{2,1,0:T(4,128)} %pad_add_fusion.windows, s32[4]{0:T(128)} %owners.1, s32[8,128]{1,0:T(8,128)} %pad.4.spots, bf16[256,128]{1,0:T(8,128)(2,1)} %constant.142.clone.tables, bf16[128,128]{1,0:T(8,128)(2,1)} %constant.143.clone.unmix, ...), custom_call_target="tpu_custom_call" | custom-call | flops 6442450944 | bytes 16777216 | tf_op jit(solution)/shard_map/pallas_call | solution.py:499
  121.9 1.7 %copy.17 = f32[4,2,8192]{2,1,0:T(2,128)} copy(f32[4,2,8192]{2,1,0:T(2,128)} %get-tuple-element.9) | data formatting | bytes 524288
  123.6 1.5 %copy.18 = f32[2,8192]{1,0:T(2,128)} copy(f32[2,8192]{1,0:T(2,128)} %get-tuple-element.10) | data formatting | bytes 131072
  (2 shorter events, 0.0 us)
Async XLA Ops:
  0.6 0.7 copy-start

commit v6 on v5

--- a/solution.py
+++ b/solution.py
@@ -14,9 +14,7 @@
 TILE_GROUP = 4
 MAP_GROUP = 4
 RAY_GROUP = 2
-SHARES = 4
-PAIR = 2
-PAIR_GAP = 2
+SHARES = 1
 
 
 def kernel_tables(side):
@@ -411,9 +409,8 @@
 
     chains = {}
     for k in range(planes):
-        begin = k // PAIR * PAIR_GAP
-        chains[k, 0] = (begin, spread_tiles(k), convolve_tiles)
-        chains[k, 1] = (begin, spread_map(k), separate)
+        chains[k, 0] = (k, spread_tiles(k), convolve_tiles)
+        chains[k, 1] = (k, spread_map(k), separate)
     jobs, left, moment = [], [2] * planes, 0
     while chains:
         for key in list(chains):
@@ -424,11 +421,10 @@
                 left[key[0]] -= 1
                 if left[key[0]] == 0:
                     jobs += [functools.partial(compute, key[0], i) for i in range(SHARES)]
-            if jobs:
-                jobs.pop(0)()
+        for job in jobs:
+            job()
+        jobs = []
         moment += 1
-    for job in jobs:
-        job()
     for copy in copies.started:
         copy.wait_send()
 

time: 125 us -> 115 us (0.920)
  Pallas kernels: 117 us -> 107 us
    pallas_call x1, Pallas kernels: 117 us -> 107 us  [per_device(): pl.pallas_call(functools.partial(body, n, nz), out_shape=[jax.ShapeDtypeS...]
where the time goes in v6:
time: 115 us
  Pallas kernels  107 us (93%)
  local copies, waits for them, and re-layouts  4.45 us (4%)
  other arithmetic  3.1 us (3%)
    pallas_call x1, Pallas kernels, per_device(): pl.pallas_call(functools.partial(body, n, nz), out_shape=[jax.ShapeDtypeS...  107 us
    unnamed x4, local copies, waits for them, and re-layouts  3.85 us

profile of v6, /device:TPU:0, one launch (start us, length us, event | category | flops | bytes accessed | tf_op | source)
XLA Modules:
  0.0 115.0 jit_solution(9495309023196860270)
XLA Ops:
  0.6 0.0 copy-start
  0.6 0.7 copy-done
  1.4 0.9 select_reduce_fusion
  2.3 0.6 pad.4.spots
  2.9 0.8 multiply_add_fusion
  3.7 0.8 multiply_subtract_fusion.1
  4.5 0.6 pad_add_fusion.windows
  5.1 106.8 %shard_map.122 = (f32[4,2,8192]{2,1,0:T(2,128)}, f32[2,8192]{1,0:T(2,128)}) custom-call(s32[4,3,16]{2,1,0:T(4,128)} %pad_add_fusion.windows, s32[4]{0:T(128)} %owners.1, s32[8,128]{1,0:T(8,128)} %pad.4.spots, bf16[256,128]{1,0:T(8,128)(2,1)} %constant.142.clone.tables, bf16[128,128]{1,0:T(8,128)(2,1)} %constant.143.clone.unmix, ...), custom_call_target="tpu_custom_call" | custom-call | flops 6442450944 | bytes 16777216 | tf_op jit(solution)/shard_map/pallas_call | solution.py:495
  111.8 1.7 %copy.17 = f32[4,2,8192]{2,1,0:T(2,128)} copy(f32[4,2,8192]{2,1,0:T(2,128)} %get-tuple-element.9) | data formatting | bytes 524288
  113.5 1.5 %copy.18 = f32[2,8192]{1,0:T(2,128)} copy(f32[2,8192]{1,0:T(2,128)} %get-tuple-element.10) | data formatting | bytes 131072
  (2 shorter events, 0.0 us)
Async XLA Ops:
  0.6 0.7 copy-start
